TPU v7x, 512 devices: a whole 4x8x8 slice. The times are simulated.
512 devices in a mesh: pipe: 32 (over y, z_hi), dp: 16 (over x, z_lo, core).
Axes of the slice: x: 4, y: 8, z: 8 (z_hi: 4, z_lo: 2; z = z_hi * 2 + z_lo), core: 2. Of those that a mesh axis runs over, the one named last changes fastest.
Arguments:
- corrected: bfloat16 [32, 2176, 6144], P('pipe', 'dp'), may hold values from -6 to 6
- inputs: bfloat16 [32, 2176, 6144], P('pipe', 'dp'), may hold values from -0.09375 to 0.09375
- act_basis: bfloat16 [32, 6144, 64], P('pipe', 'dp'), may hold values from -0.078125 to 0.078125
- weight_basis: bfloat16 [32, 6144, 64], P('pipe', 'dp'), may hold values from -0.078125 to 0.078125
Outputs:
- new_error: bfloat16 [32, 2176, 6144], P('pipe', 'dp')
- weight_right: float32 [32, 6144, 64], P('pipe', 'dp')
All inputs are finite; a program needn't handle non-finite values.
Results may differ from a plain program's by a relative error of at most 0.025.
Values may be sent and summed in bfloat16 or wider, within the bound.
No kernel may reach another device: no remote copies, remote signals or barrier semaphores. Data moves between devices by JAX's collectives and lax.ppermute only.
A program may use at most 64 MiB of HBM per device.

v0:
```python
import jax
import jax.numpy as jnp
from jax import lax
from jax.sharding import PartitionSpec as P

HIGH = lax.Precision.HIGHEST


def passed_along(shard, axis, by):
    devices = lax.axis_size(axis)
    return lax.ppermute(shard, axis, [(i, (i + by) % devices) for i in range(devices)])


def solve_with(matrix, gram_mat):
    cholesky_low = jnp.linalg.cholesky(gram_mat)
    return jax.scipy.linalg.solve_triangular(cholesky_low, matrix.T, lower=True).T


def local(corrected, inputs, act_basis, weight_basis):
    micro_rows = corrected[0]
    x_rows = inputs[0]
    basis_full, wbasis_full = (
        lax.all_gather(act_basis, "dp", axis=1, tiled=True),
        lax.all_gather(weight_basis, "dp", axis=1, tiled=True),
    )
    basis_full = basis_full[0]
    wbasis_full = wbasis_full[0]
    left_raw = jnp.dot(micro_rows, basis_full, preferred_element_type=jnp.float32)
    left_gram = jnp.dot(left_raw.T, left_raw, precision=HIGH)
    left_unit = solve_with(left_raw, left_gram).astype(jnp.bfloat16)
    right_factor = jnp.dot(micro_rows.T, left_unit, preferred_element_type=jnp.float32).astype(
        jnp.bfloat16
    )
    approx = jnp.dot(left_unit, right_factor.T, preferred_element_type=jnp.float32)
    error_rows = (micro_rows.astype(jnp.float32) - approx).astype(jnp.bfloat16)
    left_in, right_in = passed_along((left_unit, right_factor), "pipe", -1)
    left_wide = left_in.astype(jnp.float32)
    inner = jnp.dot(right_in.T, wbasis_full, preferred_element_type=jnp.float32)
    coeff = jnp.dot(left_wide, inner, precision=HIGH).astype(jnp.bfloat16)
    left_sum = lax.psum(
        jnp.dot(x_rows.T, coeff, preferred_element_type=jnp.float32).astype(jnp.bfloat16), "dp"
    ).astype(jnp.float32)
    unit_b = solve_with(left_sum, jnp.dot(left_sum.T, left_sum, precision=HIGH)).astype(
        jnp.bfloat16
    )
    middle = jnp.dot(x_rows, unit_b, preferred_element_type=jnp.float32)
    small_b = jnp.dot(left_wide.T, middle, precision=HIGH).astype(jnp.bfloat16)
    weight_out = lax.psum_scatter(
        jnp.dot(right_in, small_b, preferred_element_type=jnp.float32).astype(jnp.bfloat16),
        "dp",
        scatter_dimension=0,
        tiled=True,
    ).astype(jnp.float32)
    return (error_rows[None], weight_out[None])


def solution(mesh):
    in_specs = (
        P("pipe", "dp", None),
        P("pipe", "dp", None),
        P("pipe", "dp", None),
        P("pipe", "dp", None),
    )
    out_specs = (P("pipe", "dp", None), P("pipe", "dp", None))
    return jax.shard_map(local, mesh=mesh, in_specs=in_specs, out_specs=out_specs, check_vma=False)
```

profile of v0, /device:TPU:1, one launch (start us, length us, event | category | flops | bytes accessed | tf_op | source)
XLA Modules:
  0.0 332.2 jit_solution(10439285250637902276)
XLA Ops:
  7.2 27.8 %all_gather.6 = bf16[1,6144,64]{1,2,0:T(8,128)(2,1)S(1)} all-gather(bf16[1,384,64]{1,2,0:T(8,128)(2,1)} %param.7), channel_id=1, replica_groups=mesh['pipe'=32,'dp'=16] {'dp'}, dimensions={1}, use_global_device_ids=true | all-gather | bytes 835584 | tf_op jit(solution)/shard_map/all_gather | solution.py:23
  35.0 2.3 fusion.7
  37.6 5.8 %cholesky.44 = f32[64,64]{1,0:T(8,128)S(1)} custom-call(f32[64,64]{1,0:T(8,128)S(1)} %fusion.17), custom_call_target="Cholesky" | custom-call | tf_op jit(solution)/shard_map/jit(cholesky)/cholesky | solution.py:15
  44.2 0.7 fusion.12
  44.8 4.9 %custom-call.10 = f32[1,64,64]{1,2,0:T(8,128)S(1)} custom-call(f32[1,64,64]{2,1,0:T(8,128)S(1)} %fusion.12), custom_call_target="InvertDiagBlocksLowerTriangular" | custom-call | tf_op jit(solution)/shard_map/jit(_solve_triangular)/triangular_solve | solution.py:16
  50.5 10.7 %collective-permute-start = (bf16[6144,64]{0,1:T(8,128)(2,1)S(1)}, bf16[6144,64]{0,1:T(8,128)(2,1)S(1)}, u32[]{:S(2)}, u32[]{:S(2)}) collective-permute-start(bf16[6144,64]{0,1:T(8,128)(2,1)S(1)} %bitcast.62), channel_id=1, source_target_pairs={{0,496},{16,0},{32,16},{48,32},{64,48},{80,64},{96,80},{112,96},{1... | collective-permute-start | bytes 2359304 | tf_op jit(solution)/shard_map/ppermute | solution.py:11
  61.3 2.2 collective-permute-start.1
  63.4 45.8 %all_gather.7 = bf16[1,6144,64]{1,2,0:T(8,128)(2,1)S(1)} all-gather(bf16[1,384,64]{1,2,0:T(8,128)(2,1)S(1)} %copy-done.5), channel_id=1, replica_groups=mesh['pipe'=32,'dp'=16] {'dp'}, dimensions={1}, use_global_device_ids=true | all-gather | bytes 835584 | tf_op jit(solution)/shard_map/all_gather | solution.py:24
  109.2 0.9 copy-done.2
  110.7 1.4 fusion.2
  112.2 124.9 %all-reduce.2.cloned.1.call-done = bf16[6144,64]{0,1:T(8,128)(2,1)} async-done(((bf16[6144,64]{0,1:T(8,128)(2,1)}), bf16[6144,64]{0,1:T(8,128)(2,1)}) %all-reduce.2.cloned.1.call-update) | async-done | bytes 786448 | tf_op jit(solution)/shard_map/psum | solution.py:40
  237.1 1.7 fusion.19
  238.9 5.8 %cholesky.55 = f32[64,64]{1,0:T(8,128)S(1)} custom-call(f32[64,64]{1,0:T(8,128)S(1)} %fusion.15), custom_call_target="Cholesky" | custom-call | tf_op jit(solution)/shard_map/jit(cholesky)/cholesky | solution.py:15
  244.8 0.6 compare_reduce_fusion
  245.5 0.7 fusion.13
  246.1 4.9 %custom-call.11 = f32[1,64,64]{1,2,0:T(8,128)S(1)} custom-call(f32[1,64,64]{2,1,0:T(8,128)S(1)} %fusion.13), custom_call_target="InvertDiagBlocksLowerTriangular" | custom-call | tf_op jit(solution)/shard_map/jit(_solve_triangular)/triangular_solve | solution.py:16
  251.0 2.0 convolution_convert_fusion.3
  253.0 0.7 fusion.3
  254.1 1.3 convolution_convert_fusion.2
  255.4 2.5 copy.12
  257.9 2.9 fusion.1
  260.9 62.9 %reduce-scatter.4.cloned.1.call-done = bf16[384,64]{1,0:T(8,128)(2,1)} async-done(((bf16[6144,64]{1,0:T(8,128)(2,1)}), bf16[384,64]{1,0:T(8,128)(2,1)}) %reduce-scatter.4.cloned.1.call-update) | async-done | bytes 49168
  323.7 1.0 copy.13
  324.7 0.7 bitcast_convert_fusion
  (30 shorter events, 3.0 us)
Async XLA Ops:
  7.2 103.5 %copy-start = (bf16[1,136,6144]{2,1,0:T(8,128)(2,1)S(1)}, bf16[1,136,6144]{2,1,0:T(8,128)(2,1)}, u32[]{:S(2)}) copy-start(bf16[1,136,6144]{2,1,0:T(8,128)(2,1)} %param.6) | copy-start | bytes 5013508
  7.2 229.9 %all-reduce.2.cloned.1.call-start = ((), (), s32[]{:S(2)}) async-start(), calls=%async_computation.1 | async-start | bytes 1572864 | tf_op jit(solution)/shard_map/psum | solution.py:40
  35.0 14.9 %copy-start.1 = (bf16[1,136,6144]{2,1,0:T(8,128)(2,1)S(1)}, bf16[1,136,6144]{2,1,0:T(8,128)(2,1)}, u32[]{:S(2)}) copy-start(bf16[1,136,6144]{2,1,0:T(8,128)(2,1)} %param.5) | copy-start | bytes 5013508
  37.3 26.1 %copy-start.5 = (bf16[1,384,64]{1,2,0:T(8,128)(2,1)S(1)}, bf16[1,384,64]{1,2,0:T(8,128)(2,1)}, u32[]{:S(2)}) copy-start(bf16[1,384,64]{1,2,0:T(8,128)(2,1)} %param.8) | copy-start | bytes 147460
  50.5 60.0 %copy-start.4 = (bf16[64,6144]{1,0:T(8,128)(2,1)}, bf16[64,6144]{1,0:T(8,128)(2,1)S(1)}, u32[]{:S(2)}) copy-start(bf16[64,6144]{1,0:T(8,128)(2,1)S(1)} %convolution_convert_fusion.1) | copy-start | bytes 2359300
  50.5 58.7 %collective-permute-start = (bf16[6144,64]{0,1:T(8,128)(2,1)S(1)}, bf16[6144,64]{0,1:T(8,128)(2,1)S(1)}, u32[]{:S(2)}, u32[]{:S(2)}) collective-permute-start(bf16[6144,64]{0,1:T(8,128)(2,1)S(1)} %bitcast.62), channel_id=1, source_target_pairs={{0,496},{16,0},{32,16},{48,32},{64,48},{80,64},{96,80},{112,96},{1... | collective-permute-start | bytes 2359304 | tf_op jit(solution)/shard_map/ppermute | solution.py:11
  61.3 49.2 %collective-permute-start.1 = (bf16[136,64]{0,1:T(8,128)(2,1)S(1)}, bf16[136,64]{0,1:T(8,128)(2,1)S(1)}, u32[]{:S(2)}, u32[]{:S(2)}) collective-permute-start(bf16[136,64]{0,1:T(8,128)(2,1)S(1)} %convolution_convert_fusion.5), channel_id=1, source_target_pairs={{0,496},{16,0},{32,16},{48,32},{64,48},{80,64},{96,80},{112,96},{1... | collective-permute-start | bytes 52232 | tf_op jit(solution)/shard_map/ppermute | solution.py:11
  109.2 0.9 copy-start.2
  112.1 211.6 %reduce-scatter.4.cloned.1.call-start = ((), (), s32[]{:S(2)}) async-start(), calls=%async_computation.2 | async-start | bytes 1671168
  253.0 1.1 copy-start.3
Sparse Core Ops, SparseCore 0:
  112.3 124.8 all-reduce.1
  258.0 65.6 reduce-scatter.3
where the time goes:
time: 334 us; the launch traced here: 332 us
  waiting for transfers between devices  188 us (56%)
  blocking collectives  73.6 us (22%)
  other arithmetic  24.8 us (7%)
  between operations  14.2 us (4%)
  matrix products  14 us (4%)
  starting transfers between devices  13 us (4%)
  local copies, waits for them, and re-layouts  4.75 us (1%)
    psum x1, waiting for transfers between devices, local(): lax.psum(jnp.dot(x_rows.T, coeff, preferred_element_type=jnp.float32).ast...  125 us
    unnamed x3, waiting for transfers between devices  62.9 us
    all_gather x1, blocking collectives, local(): lax.all_gather(weight_basis, 'dp', axis=1, tiled=True)  45.8 us
    all_gather x1, blocking collectives, local(): lax.all_gather(act_basis, 'dp', axis=1, tiled=True)  27.8 us
    another operation x6, other arithmetic, solve_with(): cholesky_low = jnp.linalg.cholesky(gram_mat)  13 us
    ppermute x2, starting transfers between devices, passed_along(): lax.ppermute(shard, axis, [(i, (i + by) % devices) for i in range(devices)])  12.9 us
    another operation x4, other arithmetic, solve_with(): jax.scipy.linalg.solve_triangular(cholesky_low, matrix.T, lower=True)  11.1 us
  transfers between devices with their start and end apart: 4, of which 2 were waited for; matrix products, arithmetic and copies ran while one was open for 1% of the time, Pallas kernels for 0%

commit v1 on v0

v1 whole, which is shorter than its diff:
```python
import jax
import jax.numpy as jnp
from jax import lax
from jax.experimental import pallas as pl
from jax.experimental.pallas import tpu as pltpu
from jax.sharding import PartitionSpec as P

HIGH = lax.Precision.HIGHEST
F32, BF16 = jnp.float32, jnp.bfloat16
D, RANK, ROWS, DP = 6144, 64, 136, 16
SLICE = D // DP
ACROSS = [[2 * i + c for i in range(8)] for c in range(2)]
NT = (((1,), (1,)), ((), ()))
TN = (((0,), (0,)), ((), ()))


def passed_along(shard, axis, by):
    devices = lax.axis_size(axis)
    return lax.ppermute(shard, axis, [(i, (i + by) % devices) for i in range(devices)])


def inverse_cholesky(gram):
    wide = jnp.concatenate([gram, jnp.eye(RANK, dtype=F32)], axis=1)
    sub = lax.broadcasted_iota(jnp.int32, (8, 128), 0)
    part = [wide[8 * g : 8 * g + 8] for g in range(8)]
    for k in range(0, RANK, 4):
        own, r = divmod(k, 8)
        rows = [part[own][r + i : r + i + 1, :] for i in range(4)]
        s = [[jnp.broadcast_to(rows[i][:, k + j : k + j + 1], (1, 128)) for j in range(4)] for i in range(4)]
        done, inv, low = list(rows), [None] * 4, {}
        for i in range(4):
            inv[i] = 1.0 / s[i][i]
            for t in range(i + 1, 4):
                low[t, i] = s[i][t] * inv[i]
                for j in range(t, 4):
                    s[t][j] = s[t][j] - low[t, i] * s[i][j]
                done[t] = done[t] - low[t, i] * done[i]
        solved = [done[i] * inv[i] for i in range(4)]
        for i in (2, 1, 0):
            for t in range(i + 1, 4):
                solved[i] = solved[i] - low[t, i] * solved[t]
        for g in range(own, 8):
            if g > own or r == 0:
                less = part[g] - sum(part[g][:, k + i : k + i + 1] * solved[i] for i in range(4))
            if g > own:
                part[g] = less
            else:
                part[g] = jnp.where(sub > r + 3, less, part[g]) if r == 0 else part[g]
                for i in range(1, 4):
                    part[g] = jnp.where(sub == r + i, done[i], part[g])
    wide = jnp.concatenate(part, axis=0)
    square = (RANK, RANK)
    on_diagonal = lax.broadcasted_iota(jnp.int32, square, 0) == lax.broadcasted_iota(jnp.int32, square, 1)
    pivots = jnp.sum(jnp.where(on_diagonal, wide[:, :RANK], 0.0), axis=1, keepdims=True)
    return wide[:, RANK:] * lax.rsqrt(pivots)


def half_product(micro_ref, half_ref, core):
    total = jnp.zeros((2 * RANK, ROWS), F32)
    for i in range(DP // 2):
        at = pl.ds(pl.multiple_of((2 * i + core) * SLICE, 128), SLICE)
        total += lax.dot_general(half_ref[i], micro_ref[:, at], NT, preferred_element_type=F32)
    return total


def own_half(core_ref, micro_ref, own_ref, out_ref):
    out_ref[...] = half_product(micro_ref, own_ref, core_ref[0])


def compress(core_ref, micro_ref, other_ref, part_ref, factors_ref, right_ref):
    total = part_ref[...] + half_product(micro_ref, other_ref, 1 - core_ref[0])
    raw, warm = total[:RANK], total[RANK:]
    gram = lax.dot_general(raw, raw, NT, precision=HIGH, preferred_element_type=F32)
    left = jnp.dot(inverse_cholesky(gram), raw, precision=HIGH, preferred_element_type=F32).astype(BF16)
    inner = lax.dot_general(left.astype(F32), warm, NT, precision=HIGH, preferred_element_type=F32)
    factors_ref[...] = jnp.zeros_like(factors_ref)
    factors_ref[:, :ROWS] = left
    factors_ref[:, 192:] = inner.astype(BF16)
    for j in range(DP):
        at = slice(j * SLICE, (j + 1) * SLICE)
        right_ref[:, at] = jnp.dot(left, micro_ref[:, at], preferred_element_type=F32).astype(BF16)


def residual(micro_ref, factors_ref, right_ref, error_ref):
    left = factors_ref[:, :ROWS]
    for j in range(DP):
        at = slice(j * SLICE, (j + 1) * SLICE)
        approx = lax.dot_general(left, right_ref[:, at], TN, preferred_element_type=F32)
        error_ref[:, at] = (micro_ref[:, at].astype(F32) - approx).astype(BF16)


def project(rows_ref, factors_ref, out_ref):
    left, inner = factors_ref[:, :ROWS], factors_ref[:, 192:]
    for j in range(DP):
        at = slice(j * SLICE, (j + 1) * SLICE)
        term = jnp.dot(left, rows_ref[:, at], preferred_element_type=F32).astype(BF16)
        for c in range(3):
            out_ref[j, c * RANK : (c + 1) * RANK, :] = term[:, c * 128 : (c + 1) * 128]
        out_ref[j, 3 * RANK :, :RANK] = inner[:32]
        out_ref[j, 3 * RANK :, RANK:] = inner[32:]


def accumulate(in_ref, out_ref):
    panels = [in_ref[:, c * RANK : (c + 1) * RANK, :].reshape(DP * RANK, 128) for c in range(3)]
    terms = jnp.concatenate(panels, axis=1)
    mixed = in_ref[:, 3 * RANK :, :].reshape(DP * 32, 128)
    inner = jnp.concatenate(
        [mixed[:, :RANK].reshape(DP, 32, RANK), mixed[:, RANK:].reshape(DP, 32, RANK)], axis=1
    ).reshape(DP * RANK, RANK)
    whole = lax.dot_general(inner, terms, TN, preferred_element_type=F32)
    gram = lax.dot_general(whole, whole, NT, precision=HIGH, preferred_element_type=F32)
    high = whole.astype(BF16)
    low = (whole - high.astype(F32)).astype(BF16)
    met = lax.dot_general(high, terms, NT, preferred_element_type=F32)
    met += lax.dot_general(low, terms, NT, preferred_element_type=F32)
    for r in range(DP):
        out_ref[r, :, :RANK] = met[:, r * RANK : (r + 1) * RANK]
        out_ref[r, :, RANK:] = gram


def add_sums(in_ref, out_ref):
    total = in_ref[0]
    for j in range(1, DP):
        total += in_ref[j]
    out_ref[...] = total


def factor(in_ref, out_ref):
    out_ref[...] = inverse_cholesky(in_ref[:, RANK:])


def expand(met_ref, right_ref, out_ref):
    small = met_ref[:, :RANK].astype(BF16)
    for j in range(DP):
        at = slice(j * SLICE, (j + 1) * SLICE)
        out_ref[j] = jnp.dot(small, right_ref[:, at], preferred_element_type=F32).astype(BF16)


def add_up(in_ref, out_ref):
    total = in_ref[0].astype(F32)
    for r in range(1, DP):
        total += in_ref[r].astype(F32)
    out_ref[...] = total


VMEM = pl.BlockSpec(memory_space=pltpu.VMEM)
SMEM = pl.BlockSpec(memory_space=pltpu.SMEM)


def finish(inverse_ref, in_ref, out_ref):
    out_ref[...] = jnp.dot(inverse_ref[...], in_ref[...], precision=HIGH, preferred_element_type=F32)


def kernel(body, *shapes, flops, specs=None):
    outs = [jax.ShapeDtypeStruct(shape, dtype) for shape, dtype in shapes]
    return pl.pallas_call(
        body,
        out_shape=outs if len(outs) > 1 else outs[0],
        in_specs=specs or [VMEM] * (body.__code__.co_argcount - len(outs)),
        compiler_params=pltpu.CompilerParams(vmem_limit_bytes=32 * 2**20),
        cost_estimate=pl.CostEstimate(flops=flops, bytes_accessed=4 * 2**20, transcendentals=0),
        name=body.__name__,
    )


def local(corrected, inputs, act_basis, weight_basis):
    micro, rows = corrected[0], inputs[0]
    warm = passed_along(weight_basis[0].T, "pipe", 1)
    both = jnp.concatenate([act_basis[0].T, warm], axis=0)
    both = lax.all_to_all(
        jnp.broadcast_to(both, (8, *both.shape)), "dp", 0, 0, tiled=True, axis_index_groups=ACROSS
    )
    core = (lax.axis_index("dp") % 2).reshape(1)
    other = lax.ppermute(both, "dp", [(i, i ^ 1) for i in range(DP)])
    product = 2 * ROWS * D * RANK
    part = kernel(own_half, ((2 * RANK, ROWS), F32), flops=product, specs=[SMEM, VMEM, VMEM])(core, micro, both)
    factors, right = kernel(
        compress, ((RANK, 256), BF16), ((RANK, D), BF16), flops=2 * product, specs=[SMEM, VMEM, VMEM, VMEM]
    )(core, micro, other, part)
    factors_in = passed_along(factors, "pipe", -1)
    error = kernel(residual, ((ROWS, D), BF16), flops=product)(micro, factors, right)
    terms = kernel(project, ((DP, 224, 128), BF16), flops=product)(rows, factors_in)
    terms = lax.all_to_all(terms, "dp", 0, 0, tiled=True)
    sums = kernel(accumulate, ((DP, RANK, 128), F32), flops=product)(terms)
    sums = lax.all_to_all(sums, "dp", 0, 0, tiled=True)
    total = kernel(add_sums, ((RANK, 128), F32), flops=0)(sums)
    met = passed_along(total, "pipe", 1)
    inverse = kernel(factor, ((RANK, RANK), F32), flops=4 * product)(total)
    parts = kernel(expand, ((DP, RANK, SLICE), BF16), flops=product)(met, right)
    parts = lax.all_to_all(parts, "dp", 0, 0, tiled=True)
    parts = passed_along(kernel(add_up, ((RANK, SLICE), F32), flops=product)(parts), "pipe", -1)
    weight_right = kernel(finish, ((RANK, SLICE), F32), flops=0)(inverse, parts)
    return error[None], weight_right.T[None]


def solution(mesh):
    spec = P("pipe", "dp", None)
    return jax.shard_map(local, mesh=mesh, in_specs=(spec,) * 4, out_specs=(spec, spec), check_vma=False)
```

time: 334 us -> 121 us (0.36)
  waiting for transfers between devices: 188 us -> 19.8 us
  other arithmetic: 24.8 us -> 0.81 us
  matrix products: 14 us -> 0 us
  between operations: 14.2 us -> 0.76 us
  Pallas kernels: 0 us -> 12.7 us
  starting transfers between devices: 13 us -> 22 us
  blocking collectives: 73.6 us -> 64.7 us
  local copies, waits for them, and re-layouts: 4.75 us -> 0.08 us
    psum x1 -> x0, waiting for transfers between devices: 125 us -> none  [local(): lax.psum(jnp.dot(x_rows.T, coeff, preferred_element_type=jnp.float32).ast...]
    all_gather x2 -> x0, blocking collectives: 73.6 us -> none  [the longest x1 45.8 us: local(): lax.all_gather(weight_basis, 'dp', axis=1, tiled=True)]
    all_to_all x0 -> x4, blocking collectives: none -> 64.7 us  [the longest x1 18.4 us: local(): terms = lax.all_to_all(terms, 'dp', 0, 0, tiled=True)]
    unnamed x3 -> x0, waiting for transfers between devices: 62.9 us -> none
    another operation x10 -> x0, other arithmetic: 24.1 us -> none  [the longest x6 13 us: solve_with(): cholesky_low = jnp.linalg.cholesky(gram_mat)]
    ppermute x2 -> x4, waiting for transfers between devices: 0.01 us -> 18.4 us  [passed_along(): lax.ppermute(shard, axis, [(i, (i + by) % devices) for i in range(devices)])]
    pallas_call x0 -> x10, Pallas kernels: none -> 12.7 us  [the longest x1 4.51 us: local(): kernel(compress, ((RANK, 256), BF16), ((RANK, D), BF16), flops=2 * produc...]
    dot_general x11 -> x0, matrix products: 11.7 us -> none  [the longest x1 2.93 us: local(): jnp.dot(left_unit, right_factor.T, preferred_element_type=jnp.float32)]
  transfers between devices with their start and end apart: 4 -> 5, of which waited for: 2 -> 4; matrix products, arithmetic and copies ran while one was open for 1% -> 0% of each run, Pallas kernels for 0% -> 4%
where the time goes in v1:
time: 121 us
  blocking collectives  64.7 us (53%)
  starting transfers between devices  22 us (18%)
  waiting for transfers between devices  19.8 us (16%)
  Pallas kernels  12.7 us (10%)
    ppermute x4, waiting for transfers between devices, passed_along(): lax.ppermute(shard, axis, [(i, (i + by) % devices) for i in range(devices)])  18.4 us
    all_to_all x1, blocking collectives, local(): terms = lax.all_to_all(terms, 'dp', 0, 0, tiled=True)  18.4 us
    all_to_all x1, blocking collectives, local(): parts = lax.all_to_all(parts, 'dp', 0, 0, tiled=True)  17.3 us
    ppermute x4, starting transfers between devices, passed_along(): lax.ppermute(shard, axis, [(i, (i + by) % devices) for i in range(devices)])  17.2 us
    all_to_all x1, blocking collectives, local(): lax.all_to_all(jnp.broadcast_to(both, (8, *both.shape)), 'dp', 0, 0, tile...  15.6 us
    all_to_all x1, blocking collectives, local(): sums = lax.all_to_all(sums, 'dp', 0, 0, tiled=True)  13.5 us
    ppermute x1, starting transfers between devices, local(): other = lax.ppermute(both, 'dp', [(i, i ^ 1) for i in range(DP)])  4.78 us
    pallas_call x1, Pallas kernels, local(): kernel(compress, ((RANK, 256), BF16), ((RANK, D), BF16), flops=2 * produc...  4.51 us
  transfers between devices with their start and end apart: 5, of which 4 were waited for; matrix products, arithmetic and copies ran while one was open for 0% of the time, Pallas kernels for 4%

profile of v1, /device:TPU:1, one launch (start us, length us, event | category | flops | bytes accessed | tf_op | source)
XLA Modules:
  0.0 120.8 jit_solution(12371957337599346340)
XLA Ops:
  0.6 6.8 %collective-permute-start = (bf16[64,384]{1,0:T(8,128)(2,1)}, bf16[64,384]{1,0:T(8,128)(2,1)S(1)}, u32[]{:S(2)}, u32[]{:S(2)}) collective-permute-start(bf16[64,384]{1,0:T(8,128)(2,1)} %bitcast.20), channel_id=1, source_target_pairs={{0,16},{16,32},{32,48},{48,64},{64,80},{80,96},{96,112},{112,128},... | collective-permute-start | bytes 147464 | tf_op jit(solution)/shard_map/ppermute | solution.py:19
  7.4 10.0 %collective-permute-done = bf16[64,384]{1,0:T(8,128)(2,1)S(1)} collective-permute-done((bf16[64,384]{1,0:T(8,128)(2,1)}, bf16[64,384]{1,0:T(8,128)(2,1)S(1)}, u32[]{:S(2)}, u32[]{:S(2)}) %collective-permute-start) | collective-permute-done | bytes 49184 | tf_op jit(solution)/shard_map/ppermute | solution.py:19
  17.4 0.8 pad_maximum_fusion
  18.2 0.1 broadcast_in_dim.9
  18.3 15.6 %all_to_all.20.own_ref = bf16[8,128,384]{2,1,0:T(8,128)(2,1)S(1)} all-to-all(bf16[8,128,384]{2,1,0:T(8,128)(2,1)S(1)} %broadcast_in_dim.9), channel_id=1, replica_groups={{0,2,4,6,8,10,12,14},{1,3,5,7,9,11,13,15},{16,18,20,22,24,26,28,30},{17..., dimensions={0} | all-to-all | bytes 1572864 | tf_op jit(solution)/shard_map/all_to_all | solution.py:170
  33.8 4.8 %collective-permute-start.1 = (bf16[8,128,384]{2,1,0:T(8,128)(2,1)S(1)}, bf16[8,128,384]{2,1,0:T(8,128)(2,1)S(1)}, u32[]{:S(2)}, u32[]{:S(2)}) collective-permute-start(bf16[8,128,384]{2,1,0:T(8,128)(2,1)S(1)} %all_to_all.20.own_ref), channel_id=1, source_target_pairs={{0,1},{1,0},{2,3},{3,2},{4,5},{5,4},{6,7},{7,6},{8,9},{9,8},{10,11... | collective-permute-start | bytes 2359304 | tf_op jit(solution)/shard_map/ppermute | solution.py:174
  38.6 0.5 own_half.1.part_ref
  39.2 1.4 %collective-permute-done.1.other_ref = bf16[8,128,384]{2,1,0:T(8,128)(2,1)S(1)} collective-permute-done((bf16[8,128,384]{2,1,0:T(8,128)(2,1)S(1)}, bf16[8,128,384]{2,1,0:T(8,128)(2,1)S(1)}, u32[]{:S(2)}, u32[]{:S(2)}) %collective-permute-start.1) | collective-permute-done | bytes 786464 | tf_op jit(solution)/shard_map/ppermute | solution.py:174
  40.5 4.5 %compress.1 = (bf16[64,256]{1,0:T(8,128)(2,1)S(1)}, bf16[64,6144]{1,0:T(8,128)(2,1)S(1)}) custom-call(s32[1]{0:T(128)} %bitcast.1.core_ref, bf16[136,6144]{1,0:T(8,128)(2,1)S(1)} %bitcast.14, bf16[8,128,384]{2,1,0:T(8,128)(2,1)S(1)} %collective-permute-done.1.other_ref, f32[128,136]{1,0:T(8,128)S(1)} %own_half.1.part_ref), custom_call_target="tpu_custom_call" | custom-call | flops 213909504 | bytes 4194304 | tf_op jit(solution)/shard_map/compress/pallas_call | solution.py:177
  45.0 4.4 %collective-permute-start.2 = (bf16[64,256]{1,0:T(8,128)(2,1)S(1)}, bf16[64,256]{1,0:T(8,128)(2,1)S(1)}, u32[]{:S(2)}, u32[]{:S(2)}) collective-permute-start(bf16[64,256]{1,0:T(8,128)(2,1)S(1)} %get-tuple-element.4.factors_ref), channel_id=1, source_target_pairs={{0,496},{16,0},{32,16},{48,32},{64,48},{80,64},{96,80},{112,96},{1... | collective-permute-start | bytes 98312 | tf_op jit(solution)/shard_map/ppermute | solution.py:19
  49.4 1.2 collective-permute-done.2.factors_ref
  50.7 0.5 project.1
  51.1 18.4 %all_to_all.21.in_ref = bf16[16,224,128]{2,1,0:T(8,128)(2,1)S(1)} all-to-all(bf16[16,224,128]{2,1,0:T(8,128)(2,1)S(1)} %project.1), channel_id=1, replica_groups=mesh['pipe'=32,'dp'=16] {'dp'}, dimensions={0} | all-to-all | bytes 1835008 | tf_op jit(solution)/shard_map/all_to_all | solution.py:183
  69.5 1.1 accumulate.1
  70.6 13.5 %all_to_all.22.in_ref = f32[16,64,128]{2,1,0:T(8,128)S(1)} all-to-all(f32[16,64,128]{2,1,0:T(8,128)S(1)} %accumulate.1), channel_id=1, replica_groups=mesh['pipe'=32,'dp'=16] {'dp'}, dimensions={0} | all-to-all | bytes 1048576 | tf_op jit(solution)/shard_map/all_to_all | solution.py:185
  84.1 1.9 %collective-permute-start.3 = (f32[64,128]{1,0:T(8,128)S(1)}, f32[64,128]{1,0:T(8,128)S(1)}, u32[]{:S(2)}, u32[]{:S(2)}) collective-permute-start(f32[64,128]{1,0:T(8,128)S(1)} %add_sums.1.in_ref), channel_id=1, source_target_pairs={{0,16},{16,32},{32,48},{48,64},{64,80},{80,96},{96,112},{112,128},... | collective-permute-start | bytes 98312 | tf_op jit(solution)/shard_map/ppermute | solution.py:19
  86.1 7.2 %collective-permute-done.3.met_ref = f32[64,128]{1,0:T(8,128)S(1)} collective-permute-done((f32[64,128]{1,0:T(8,128)S(1)}, f32[64,128]{1,0:T(8,128)S(1)}, u32[]{:S(2)}, u32[]{:S(2)}) %collective-permute-start.3) | collective-permute-done | bytes 32800 | tf_op jit(solution)/shard_map/ppermute | solution.py:19
  93.3 0.4 expand.1
  93.7 17.3 %all_to_all.23.in_ref = bf16[16,64,384]{2,1,0:T(8,128)(2,1)S(1)} all-to-all(bf16[16,64,384]{2,1,0:T(8,128)(2,1)S(1)} %expand.1), channel_id=1, replica_groups=mesh['pipe'=32,'dp'=16] {'dp'}, dimensions={0} | all-to-all | bytes 1572864 | tf_op jit(solution)/shard_map/all_to_all | solution.py:190
  111.0 0.1 add_up.1
  111.1 4.1 %collective-permute-start.4 = (f32[64,384]{1,0:T(8,128)S(1)}, f32[64,384]{1,0:T(8,128)S(1)}, u32[]{:S(2)}, u32[]{:S(2)}) collective-permute-start(f32[64,384]{1,0:T(8,128)S(1)} %add_up.1), channel_id=1, source_target_pairs={{0,496},{16,0},{32,16},{48,32},{64,48},{80,64},{96,80},{112,96},{1... | collective-permute-start | bytes 294920 | tf_op jit(solution)/shard_map/ppermute | solution.py:19
  115.2 2.0 %residual.1 = bf16[136,6144]{1,0:T(8,128)(2,1)} custom-call(bf16[136,6144]{1,0:T(8,128)(2,1)S(1)} %bitcast.15, bf16[64,256]{1,0:T(8,128)(2,1)S(1)} %get-tuple-element.4.factors_ref, bf16[64,6144]{1,0:T(8,128)(2,1)S(1)} %get-tuple-element.5.right_ref), custom_call_target="tpu_custom_call" | custom-call | flops 106954752 | bytes 4194304 | tf_op jit(solution)/shard_map/residual/pallas_call | solution.py:181
  117.2 2.8 %factor.1.inverse_ref = f32[64,64]{1,0:T(8,128)S(1)} custom-call(f32[64,128]{1,0:T(8,128)S(1)} %add_sums.1.in_ref), custom_call_target="tpu_custom_call" | custom-call | flops 427819008 | bytes 4194304 | tf_op jit(solution)/shard_map/factor/pallas_call | solution.py:188
  120.0 0.9 finish.1
  (6 shorter events, 0.0 us)
Async XLA Ops:
  0.6 38.0 %copy-start = (bf16[1,136,6144]{2,1,0:T(8,128)(2,1)S(1)}, bf16[1,136,6144]{2,1,0:T(8,128)(2,1)}, u32[]{:S(2)}) copy-start(bf16[1,136,6144]{2,1,0:T(8,128)(2,1)} %param.4) | copy-start | bytes 5013508
  0.6 16.7 %collective-permute-start = (bf16[64,384]{1,0:T(8,128)(2,1)}, bf16[64,384]{1,0:T(8,128)(2,1)S(1)}, u32[]{:S(2)}, u32[]{:S(2)}) collective-permute-start(bf16[64,384]{1,0:T(8,128)(2,1)} %bitcast.20), channel_id=1, source_target_pairs={{0,16},{16,32},{32,48},{48,64},{64,80},{80,96},{96,112},{112,128},... | collective-permute-start | bytes 147464 | tf_op jit(solution)/shard_map/ppermute | solution.py:19
  33.8 6.7 %collective-permute-start.1 = (bf16[8,128,384]{2,1,0:T(8,128)(2,1)S(1)}, bf16[8,128,384]{2,1,0:T(8,128)(2,1)S(1)}, u32[]{:S(2)}, u32[]{:S(2)}) collective-permute-start(bf16[8,128,384]{2,1,0:T(8,128)(2,1)S(1)} %all_to_all.20.own_ref), channel_id=1, source_target_pairs={{0,1},{1,0},{2,3},{3,2},{4,5},{5,4},{6,7},{7,6},{8,9},{9,8},{10,11... | collective-permute-start | bytes 2359304 | tf_op jit(solution)/shard_map/ppermute | solution.py:174
  39.1 11.5 %copy-start.1 = (bf16[1,136,6144]{2,1,0:T(8,128)(2,1)S(1)}, bf16[1,136,6144]{2,1,0:T(8,128)(2,1)}, u32[]{:S(2)}) copy-start(bf16[1,136,6144]{2,1,0:T(8,128)(2,1)} %param.5) | copy-start | bytes 5013508
  45.0 5.6 %collective-permute-start.2 = (bf16[64,256]{1,0:T(8,128)(2,1)S(1)}, bf16[64,256]{1,0:T(8,128)(2,1)S(1)}, u32[]{:S(2)}, u32[]{:S(2)}) collective-permute-start(bf16[64,256]{1,0:T(8,128)(2,1)S(1)} %get-tuple-element.4.factors_ref), channel_id=1, source_target_pairs={{0,496},{16,0},{32,16},{48,32},{64,48},{80,64},{96,80},{112,96},{1... | collective-permute-start | bytes 98312 | tf_op jit(solution)/shard_map/ppermute | solution.py:19
  84.1 9.2 %collective-permute-start.3 = (f32[64,128]{1,0:T(8,128)S(1)}, f32[64,128]{1,0:T(8,128)S(1)}, u32[]{:S(2)}, u32[]{:S(2)}) collective-permute-start(f32[64,128]{1,0:T(8,128)S(1)} %add_sums.1.in_ref), channel_id=1, source_target_pairs={{0,16},{16,32},{32,48},{48,64},{64,80},{80,96},{96,112},{112,128},... | collective-permute-start | bytes 98312 | tf_op jit(solution)/shard_map/ppermute | solution.py:19
  111.1 8.9 %collective-permute-start.4 = (f32[64,384]{1,0:T(8,128)S(1)}, f32[64,384]{1,0:T(8,128)S(1)}, u32[]{:S(2)}, u32[]{:S(2)}) collective-permute-start(f32[64,384]{1,0:T(8,128)S(1)} %add_up.1), channel_id=1, source_target_pairs={{0,496},{16,0},{32,16},{48,32},{64,48},{80,64},{96,80},{112,96},{1... | collective-permute-start | bytes 294920 | tf_op jit(solution)/shard_map/ppermute | solution.py:19

commit v2 on v1

v2 whole, which is shorter than its diff:
```python
import jax
import jax.numpy as jnp
from jax import lax
from jax.experimental import pallas as pl
from jax.experimental.pallas import tpu as pltpu
from jax.sharding import PartitionSpec as P

HIGH = lax.Precision.HIGHEST
F32, BF16 = jnp.float32, jnp.bfloat16
D, RANK, ROWS, DP = 6144, 64, 136, 16
SLICE = D // DP
HALF = DP // 2
CORES = [[2 * i, 2 * i + 1] for i in range(HALF)]
ACROSS = [[2 * i + c for i in range(HALF)] for c in range(2)]
NT = (((1,), (1,)), ((), ()))
TN = (((0,), (0,)), ((), ()))


def passed_along(shard, by):
    devices = lax.axis_size("pipe")
    return lax.ppermute(shard, "pipe", [(i, (i + by) % devices) for i in range(devices)])


def exchanged(shard):
    return lax.ppermute(shard, "dp", [(i, i ^ 1) for i in range(DP)])


def both_cores(shard):
    return lax.all_gather(shard, "dp", axis_index_groups=CORES)


def across(blocks):
    return lax.all_to_all(blocks, "dp", 0, 0, tiled=True, axis_index_groups=ACROSS)


def strip(i, core):
    return pl.ds(pl.multiple_of((2 * i + core) * SLICE, 128), SLICE)


def inverse_cholesky(gram):
    wide = jnp.concatenate([gram, jnp.eye(RANK, dtype=F32)], axis=1)
    sub = lax.broadcasted_iota(jnp.int32, (8, 128), 0)
    part = [wide[8 * g : 8 * g + 8] for g in range(8)]
    for k in range(0, RANK, 4):
        own, r = divmod(k, 8)
        rows = [part[own][r + i : r + i + 1, :] for i in range(4)]
        s = [[jnp.broadcast_to(rows[i][:, k + j : k + j + 1], (1, 128)) for j in range(4)] for i in range(4)]
        done, inv, low = list(rows), [None] * 4, {}
        for i in range(4):
            inv[i] = 1.0 / s[i][i]
            for t in range(i + 1, 4):
                low[t, i] = s[i][t] * inv[i]
                for j in range(t, 4):
                    s[t][j] = s[t][j] - low[t, i] * s[i][j]
                done[t] = done[t] - low[t, i] * done[i]
        solved = [done[i] * inv[i] for i in range(4)]
        for i in (2, 1, 0):
            for t in range(i + 1, 4):
                solved[i] = solved[i] - low[t, i] * solved[t]
        for g in range(own, 8):
            if g > own or r == 0:
                less = part[g] - sum(part[g][:, k + i : k + i + 1] * solved[i] for i in range(4))
            if g > own:
                part[g] = less
            else:
                part[g] = jnp.where(sub > r + 3, less, part[g]) if r == 0 else part[g]
                for i in range(1, 4):
                    part[g] = jnp.where(sub == r + i, done[i], part[g])
    wide = jnp.concatenate(part, axis=0)
    square = (RANK, RANK)
    on_diagonal = lax.broadcasted_iota(jnp.int32, square, 0) == lax.broadcasted_iota(jnp.int32, square, 1)
    pivots = jnp.sum(jnp.where(on_diagonal, wide[:, :RANK], 0.0), axis=1, keepdims=True)
    return wide[:, RANK:] * lax.rsqrt(pivots)


def split_halves(core_ref, in_ref, own_ref, other_ref):
    core = core_ref[0]
    for i in range(HALF):
        own_ref[i] = in_ref[:, strip(i, core)]
        other_ref[i] = in_ref[:, strip(i, 1 - core)]


def copies(one_ref, two_ref, out_ref):
    for i in range(HALF):
        out_ref[i, :RANK, :] = one_ref[...]
        out_ref[i, RANK:, :] = two_ref[...]


def half_product(core_ref, own_ref, other_ref, both_ref, out_ref):
    core = core_ref[0]
    own, other = jnp.zeros((ROWS, 2 * RANK), F32), jnp.zeros((ROWS, 2 * RANK), F32)
    for i in range(HALF):
        own += lax.dot_general(own_ref[i], both_ref[i], NT, preferred_element_type=F32)
        other += lax.dot_general(other_ref[i], both_ref[i], NT, preferred_element_type=F32)
    out_ref[core] = own
    out_ref[1 - core] = other


def factors_of(parts_ref, out_ref):
    total = [(parts_ref[0, slot] + parts_ref[1, slot]).T for slot in range(2)]
    raw = [both[:RANK] for both in total]
    gram = [lax.dot_general(a, a, NT, precision=HIGH, preferred_element_type=F32) for a in raw]
    inverse = [inverse_cholesky(a) for a in gram]
    for slot in range(2):
        left = jnp.dot(inverse[slot], raw[slot], precision=HIGH, preferred_element_type=F32).astype(BF16)
        inner = lax.dot_general(
            left.astype(F32), total[slot][RANK:], NT, precision=HIGH, preferred_element_type=F32
        )
        out_ref[slot] = jnp.zeros((RANK, 256), BF16)
        out_ref[slot, :, :ROWS] = left
        out_ref[slot, :, 192:] = inner.astype(BF16)


def against(core_ref, own_ref, other_ref, factors_ref, out_ref):
    core = core_ref[0]
    own, other = factors_ref[core, :, :ROWS], factors_ref[1 - core, :, :ROWS]
    at, to = pl.multiple_of(core * RANK, RANK), pl.multiple_of((1 - core) * RANK, RANK)
    for i in range(HALF):
        out_ref[i, pl.ds(at, RANK), :] = jnp.dot(
            own, own_ref[i], preferred_element_type=F32
        ).astype(BF16)
        out_ref[i, pl.ds(to, RANK), :] = jnp.dot(other, other_ref[i], preferred_element_type=F32).astype(BF16)


def project(core_ref, own_ref, other_ref, factors_ref, out_ref, term_ref):
    against(core_ref, own_ref, other_ref, factors_ref, out_ref)
    inner = jnp.concatenate([factors_ref[0, :, 192:], factors_ref[1, :, 192:]], axis=0)
    for i in range(HALF):
        term_ref[i] = lax.dot_general(inner, out_ref[i], TN, preferred_element_type=F32).astype(BF16)


def residual(core_ref, micro_ref, factors_ref, error_ref):
    left = factors_ref[core_ref[0], :, :ROWS]
    upright = left.astype(F32).T.astype(BF16)
    for j in range(DP):
        micro = micro_ref[:, j * SLICE : (j + 1) * SLICE]
        right = jnp.dot(left, micro, preferred_element_type=F32).astype(BF16)
        approx = jnp.dot(upright, right, preferred_element_type=F32)
        error_ref[:, j * SLICE : (j + 1) * SLICE] = (micro.astype(F32) - approx).astype(BF16)


def add_up(in_ref, out_ref):
    total = in_ref[0].astype(F32)
    for i in range(1, HALF):
        total += in_ref[i].astype(F32)
    out_ref[...] = total


def add_and_copy(in_ref, out_ref):
    total = in_ref[0].astype(F32)
    for i in range(1, HALF):
        total += in_ref[i].astype(F32)
    for i in range(HALF):
        out_ref[i] = total.astype(BF16)


def meet(whole_ref, terms_ref, out_ref):
    met, gram = jnp.zeros((RANK, 2 * RANK), F32), jnp.zeros((RANK, RANK), F32)
    for i in range(HALF):
        met += lax.dot_general(whole_ref[i], terms_ref[i], NT, preferred_element_type=F32)
        gram += lax.dot_general(whole_ref[i], whole_ref[i], NT, preferred_element_type=F32)
    out_ref[:, : 2 * RANK] = met
    out_ref[:, 2 * RANK : 3 * RANK] = gram
    out_ref[:, 3 * RANK :] = jnp.zeros((RANK, RANK), F32)


def add_met(parts_ref, out_ref):
    out_ref[...] = parts_ref[0, :, : 2 * RANK] + parts_ref[1, :, : 2 * RANK]


def factor(parts_ref, out_ref):
    at = slice(2 * RANK, 3 * RANK)
    out_ref[...] = inverse_cholesky(parts_ref[0, :, at] + parts_ref[1, :, at])


def expand(met_ref, right_ref, out_ref):
    met = met_ref[...].astype(BF16)
    for i in range(HALF):
        out_ref[i] = jnp.dot(met, right_ref[i], preferred_element_type=F32).astype(BF16)


def finish(inverse_ref, in_ref, out_ref):
    out_ref[...] = jnp.dot(inverse_ref[...], in_ref[...], precision=HIGH, preferred_element_type=F32)


VMEM = pl.BlockSpec(memory_space=pltpu.VMEM)
SMEM = pl.BlockSpec(memory_space=pltpu.SMEM)


def kernel(body, *shapes, flops=0):
    outs = [jax.ShapeDtypeStruct(shape, dtype) for shape, dtype in shapes]
    names = body.__code__.co_varnames[: body.__code__.co_argcount - len(outs)]
    return pl.pallas_call(
        body,
        out_shape=outs if len(outs) > 1 else outs[0],
        in_specs=[SMEM if name == "core_ref" else VMEM for name in names],
        compiler_params=pltpu.CompilerParams(vmem_limit_bytes=32 * 2**20),
        cost_estimate=pl.CostEstimate(flops=flops, bytes_accessed=2**20, transcendentals=0),
        name=body.__name__,
    )


def local(corrected, inputs, act_basis, weight_basis):
    micro, rows = corrected[0], inputs[0]
    core = (lax.axis_index("dp") % 2).reshape(1)
    product = 2 * ROWS * D * RANK
    halves = ((HALF, ROWS, SLICE), BF16)
    stacked = ((HALF, 2 * RANK, SLICE), BF16)
    blocks = ((HALF, RANK, SLICE), BF16)

    warm = passed_along(weight_basis[0].T, 1)
    both = across(kernel(copies, stacked)(act_basis[0].T, warm))
    micro_own, micro_other = kernel(split_halves, halves, halves)(core, micro)
    micro_other = exchanged(micro_other)
    rows_own, rows_other = kernel(split_halves, halves, halves)(core, rows)
    rows_other = exchanged(rows_other)
    part = kernel(half_product, ((2, ROWS, 2 * RANK), F32), flops=2 * product)(core, micro_own, micro_other, both)
    factors = kernel(factors_of, ((2, RANK, 256), BF16), flops=4 * product)(both_cores(part))
    factors_in = passed_along(factors, -1)
    error = kernel(residual, ((ROWS, D), BF16), flops=2 * product)(core, micro, factors)
    factors_in, error = lax.optimization_barrier((factors_in, error))
    right = kernel(against, stacked, flops=product)(core, micro_own, micro_other, factors)
    terms, summed = kernel(project, stacked, blocks, flops=product)(core, rows_own, rows_other, factors_in)
    whole = across(kernel(add_and_copy, blocks)(across(summed)))
    met = both_cores(kernel(meet, ((RANK, 256), F32), flops=product)(whole, terms))
    met_in = passed_along(kernel(add_met, ((RANK, 2 * RANK), F32))(met), 1)
    parts = across(kernel(expand, blocks, flops=product)(met_in, right))
    parts = passed_along(kernel(add_up, ((RANK, SLICE), F32))(parts), -1)
    inverse = kernel(factor, ((RANK, RANK), F32), flops=4 * product)(met)
    weight_right = kernel(finish, ((RANK, SLICE), F32))(inverse, parts)
    return error[None], weight_right.T[None]


def solution(mesh):
    spec = P("pipe", "dp", None)
    return jax.shard_map(local, mesh=mesh, in_specs=(spec,) * 4, out_specs=(spec, spec), check_vma=False)
```

time: 121 us -> 110 us (0.909)
  the two profiles are of different devices: /device:TPU:1 before, /device:TPU:2 now
where the time goes in v2:
time: 110 us
  blocking collectives  38.1 us (35%)
  starting transfers between devices  24.9 us (23%)
  waiting for transfers between devices  23.7 us (22%)
  Pallas kernels  19.1 us (17%)
  local copies, waits for them, and re-layouts  3.17 us (3%)
    all_to_all x3, blocking collectives, across(): lax.all_to_all(blocks, 'dp', 0, 0, tiled=True, axis_index_groups=ACROSS)  34.2 us
    ppermute x4, waiting for transfers between devices, passed_along(): lax.ppermute(shard, 'pipe', [(i, (i + by) % devices) for i in range(devic...  21.7 us
    ppermute x4, starting transfers between devices, passed_along(): lax.ppermute(shard, 'pipe', [(i, (i + by) % devices) for i in range(devic...  15 us
    all_to_all x1, starting transfers between devices, across(): lax.all_to_all(blocks, 'dp', 0, 0, tiled=True, axis_index_groups=ACROSS)  5.56 us
    ppermute x2, starting transfers between devices, exchanged(): return lax.ppermute(shard, 'dp', [(i, i ^ 1) for i in range(DP)])  4.32 us
    pallas_call x1, Pallas kernels, local(): kernel(residual, ((ROWS, D), BF16), flops=2 * product)(core, micro, factors)  4.26 us
    all_gather x2, blocking collectives, both_cores(): return lax.all_gather(shard, 'dp', axis_index_groups=CORES)  3.91 us
    pallas_call x1, Pallas kernels, local(): kernel(factors_of, ((2, RANK, 256), BF16), flops=4 * product)  3.79 us
  transfers between devices with their start and end apart: 7, of which 4 were waited for; matrix products, arithmetic and copies ran while one was open for 0% of the time, Pallas kernels for 13%

profile of v2, /device:TPU:2, one launch (start us, length us, event | category | flops | bytes accessed | tf_op | source)
XLA Modules:
  0.0 109.7 jit_solution(17885245799383070748)
XLA Ops:
  0.6 6.2 %collective-permute-start.1 = (bf16[64,384]{1,0:T(8,128)(2,1)}, bf16[64,384]{1,0:T(8,128)(2,1)S(1)}, u32[]{:S(2)}, u32[]{:S(2)}) collective-permute-start(bf16[64,384]{1,0:T(8,128)(2,1)} %bitcast.24), channel_id=1, source_target_pairs={{0,16},{16,32},{32,48},{48,64},{64,80},{80,96},{96,112},{112,128},... | collective-permute-start | bytes 147464 | tf_op jit(solution)/shard_map/ppermute | solution.py:21
  6.9 10.7 %collective-permute-done.1.two_ref = bf16[64,384]{1,0:T(8,128)(2,1)S(1)} collective-permute-done((bf16[64,384]{1,0:T(8,128)(2,1)}, bf16[64,384]{1,0:T(8,128)(2,1)S(1)}, u32[]{:S(2)}, u32[]{:S(2)}) %collective-permute-start.1) | collective-permute-done | bytes 49184 | tf_op jit(solution)/shard_map/ppermute | solution.py:21
  18.4 0.9 copies.1
  19.4 5.6 %all-to-all-start = ((bf16[8,128,384]{2,1,0:T(8,128)(2,1)}), bf16[8,128,384]{2,1,0:T(8,128)(2,1)}, u32[]{:S(2)}, u32[]{:S(2)}) async-start(bf16[8,128,384]{2,1,0:T(8,128)(2,1)} %copies.1), calls=%async_computation | async-start | bytes 1572864 | tf_op jit(solution)/shard_map/all_to_all | solution.py:33
  25.1 1.9 %collective-permute-start = (bf16[8,136,384]{2,1,0:T(8,128)(2,1)S(1)}, bf16[8,136,384]{2,1,0:T(8,128)(2,1)S(1)}, u32[]{:S(2)}, u32[]{:S(2)}) collective-permute-start(bf16[8,136,384]{2,1,0:T(8,128)(2,1)S(1)} %get-tuple-element.11), channel_id=1, source_target_pairs={{0,1},{1,0},{2,3},{3,2},{4,5},{5,4},{6,7},{7,6},{8,9},{9,8},{10,11... | collective-permute-start | bytes 2506760 | tf_op jit(solution)/shard_map/ppermute | solution.py:25
  27.0 1.4 %copy-done.1 = bf16[1,136,6144]{2,1,0:T(8,128)(2,1)S(1)} copy-done((bf16[1,136,6144]{2,1,0:T(8,128)(2,1)S(1)}, bf16[1,136,6144]{2,1,0:T(8,128)(2,1)}, u32[]{:S(2)}) %copy-start.1) | copy-done | bytes 1671192
  28.5 1.1 split_halves.3
  30.4 2.4 %collective-permute-start.3 = (bf16[8,136,384]{2,1,0:T(8,128)(2,1)}, bf16[8,136,384]{2,1,0:T(8,128)(2,1)}, u32[]{:S(2)}, u32[]{:S(2)}) collective-permute-start(bf16[8,136,384]{2,1,0:T(8,128)(2,1)} %get-tuple-element.14), channel_id=1, source_target_pairs={{0,1},{1,0},{2,3},{3,2},{4,5},{5,4},{6,7},{7,6},{8,9},{9,8},{10,11... | collective-permute-start | bytes 2506760 | tf_op jit(solution)/shard_map/ppermute | solution.py:25
  32.9 2.0 %all-to-all-done.both_ref = bf16[8,128,384]{2,1,0:T(8,128)(2,1)} async-done(((bf16[8,128,384]{2,1,0:T(8,128)(2,1)}), bf16[8,128,384]{2,1,0:T(8,128)(2,1)}, u32[]{:S(2)}, u32[]{:S(2)}) %all-to-all-start) | async-done | bytes 786464 | tf_op jit(solution)/shard_map/all_to_all | solution.py:33
  34.9 1.9 %half_product.1 = f32[2,136,128]{2,1,0:T(8,128)S(1)} custom-call(s32[1]{0:T(128)} %bitcast.core_ref, bf16[8,136,384]{2,1,0:T(8,128)(2,1)S(1)} %get-tuple-element.10.own_ref, bf16[8,136,384]{2,1,0:T(8,128)(2,1)S(1)} %collective-permute-done.other_ref, bf16[8,128,384]{2,1,0:T(8,128)(2,1)} %all-to-all-done.both_ref), custom_call_target="tpu_custom_call" | custom-call | flops 213909504 | bytes 1048576 | tf_op jit(solution)/shard_map/half_product/pallas_call | solution.py:217
  36.8 2.0 %all-gather = f32[4,136,128]{2,1,0:T(8,128)S(1)} all-gather(f32[2,136,128]{2,1,0:T(8,128)S(1)} %half_product.1), channel_id=2, replica_groups={{0,1},{2,3},{4,5},{6,7},{8,9},{10,11},{12,13},{14,15},{16,17},{18,19},{..., dimensions={0}, use_global_device_ids=true | all-gather | bytes 417792 | tf_op jit(solution)/shard_map/all_gather | solution.py:29
  38.8 3.8 %factors_of.1.factors_ref = bf16[2,64,256]{2,1,0:T(8,128)(2,1)S(1)} custom-call(f32[2,2,136,128]{3,2,1,0:T(8,128)S(1)} %bitcast.20), custom_call_target="tpu_custom_call" | custom-call | flops 427819008 | bytes 1048576 | tf_op jit(solution)/shard_map/factors_of/pallas_call | solution.py:218
  42.6 4.8 %collective-permute-start.2 = (bf16[2,64,256]{2,1,0:T(8,128)(2,1)S(1)}, bf16[2,64,256]{2,1,0:T(8,128)(2,1)S(1)}, u32[]{:S(2)}, u32[]{:S(2)}) collective-permute-start(bf16[2,64,256]{2,1,0:T(8,128)(2,1)S(1)} %factors_of.1.factors_ref), channel_id=1, source_target_pairs={{0,496},{16,0},{32,16},{48,32},{64,48},{80,64},{96,80},{112,96},{1... | collective-permute-start | bytes 196616 | tf_op jit(solution)/shard_map/ppermute | solution.py:21
  47.3 4.3 %residual.1 = bf16[136,6144]{1,0:T(8,128)(2,1)} custom-call(s32[1]{0:T(128)} %bitcast.core_ref, bf16[136,6144]{1,0:T(8,128)(2,1)S(1)} %bitcast.16, bf16[2,64,256]{2,1,0:T(8,128)(2,1)S(1)} %factors_of.1.factors_ref), custom_call_target="tpu_custom_call" | custom-call | flops 213909504 | bytes 1048576 | tf_op jit(solution)/shard_map/residual/pallas_call | solution.py:220
  51.6 1.9 %project.1 = (bf16[8,128,384]{2,1,0:T(8,128)(2,1)S(1)}, bf16[8,64,384]{2,1,0:T(8,128)(2,1)S(1)}) custom-call(s32[1]{0:T(128)} %bitcast.core_ref, bf16[8,136,384]{2,1,0:T(8,128)(2,1)S(1)} %copy-done.3, bf16[8,136,384]{2,1,0:T(8,128)(2,1)} %collective-permute-done.3.other_ref, bf16[2,64,256]{2,1,0:T(8,128)(2,1)S(1)} %collective-permute-done.2.factors_ref), custom_call_target="tpu_custom_call" | custom-call | flops 106954752 | bytes 1048576 | tf_op jit(solution)/shard_map/project/pallas_call | solution.py:223
  53.5 12.0 %all_to_all.20.in_ref = bf16[8,64,384]{2,1,0:T(8,128)(2,1)S(1)} all-to-all(bf16[8,64,384]{2,1,0:T(8,128)(2,1)S(1)} %get-tuple-element.16), channel_id=1, replica_groups={{0,2,4,6,8,10,12,14},{1,3,5,7,9,11,13,15},{16,18,20,22,24,26,28,30},{17..., dimensions={0} | all-to-all | bytes 786432 | tf_op jit(solution)/shard_map/all_to_all | solution.py:33
  65.6 10.6 %all_to_all.21.whole_ref = bf16[8,64,384]{2,1,0:T(8,128)(2,1)S(1)} all-to-all(bf16[8,64,384]{2,1,0:T(8,128)(2,1)S(1)} %add_and_copy.1), channel_id=1, replica_groups={{0,2,4,6,8,10,12,14},{1,3,5,7,9,11,13,15},{16,18,20,22,24,26,28,30},{17..., dimensions={0} | all-to-all | bytes 786432 | tf_op jit(solution)/shard_map/all_to_all | solution.py:33
  76.8 1.9 %all-gather.1 = f32[128,256]{1,0:T(8,128)S(1)} all-gather(f32[64,256]{1,0:T(8,128)S(1)} %meet.1), channel_id=3, replica_groups={{0,1},{2,3},{4,5},{6,7},{8,9},{10,11},{12,13},{14,15},{16,17},{18,19},{..., dimensions={0}, use_global_device_ids=true | all-gather | bytes 196608 | tf_op jit(solution)/shard_map/all_gather | solution.py:29
  78.8 2.1 %collective-permute-start.4 = (f32[64,128]{1,0:T(8,128)S(1)}, f32[64,128]{1,0:T(8,128)S(1)}, u32[]{:S(2)}, u32[]{:S(2)}) collective-permute-start(f32[64,128]{1,0:T(8,128)S(1)} %add_met.1), channel_id=1, source_target_pairs={{0,16},{16,32},{32,48},{48,64},{64,80},{80,96},{96,112},{112,128},... | collective-permute-start | bytes 98312 | tf_op jit(solution)/shard_map/ppermute | solution.py:21
  81.3 7.4 %collective-permute-done.4.met_ref = f32[64,128]{1,0:T(8,128)S(1)} collective-permute-done((f32[64,128]{1,0:T(8,128)S(1)}, f32[64,128]{1,0:T(8,128)S(1)}, u32[]{:S(2)}, u32[]{:S(2)}) %collective-permute-start.4) | collective-permute-done | bytes 32800 | tf_op jit(solution)/shard_map/ppermute | solution.py:21
  89.1 11.5 %all_to_all.22.in_ref = bf16[8,64,384]{2,1,0:T(8,128)(2,1)S(1)} all-to-all(bf16[8,64,384]{2,1,0:T(8,128)(2,1)S(1)} %expand.1), channel_id=1, replica_groups={{0,2,4,6,8,10,12,14},{1,3,5,7,9,11,13,15},{16,18,20,22,24,26,28,30},{17..., dimensions={0} | all-to-all | bytes 786432 | tf_op jit(solution)/shard_map/all_to_all | solution.py:33
  100.6 2.0 %collective-permute-start.5 = (f32[64,384]{1,0:T(8,128)S(1)}, f32[64,384]{1,0:T(8,128)S(1)}, u32[]{:S(2)}, u32[]{:S(2)}) collective-permute-start(f32[64,384]{1,0:T(8,128)S(1)} %add_up.1), channel_id=1, source_target_pairs={{0,496},{16,0},{32,16},{48,32},{64,48},{80,64},{96,80},{112,96},{1... | collective-permute-start | bytes 294920 | tf_op jit(solution)/shard_map/ppermute | solution.py:21
  102.6 2.7 %factor.1.inverse_ref = f32[64,64]{1,0:T(8,128)S(1)} custom-call(f32[2,64,256]{2,1,0:T(8,128)S(1)} %bitcast.19), custom_call_target="tpu_custom_call" | custom-call | flops 427819008 | bytes 1048576 | tf_op jit(solution)/shard_map/factor/pallas_call | solution.py:229
  105.3 3.5 %collective-permute-done.5.in_ref = f32[64,384]{1,0:T(8,128)S(1)} collective-permute-done((f32[64,384]{1,0:T(8,128)S(1)}, f32[64,384]{1,0:T(8,128)S(1)}, u32[]{:S(2)}, u32[]{:S(2)}) %collective-permute-start.5) | collective-permute-done | bytes 98336 | tf_op jit(solution)/shard_map/ppermute | solution.py:21
  (20 shorter events, 4.2 us)
Async XLA Ops:
  0.6 24.3 %copy-start = (bf16[1,136,6144]{2,1,0:T(8,128)(2,1)S(1)}, bf16[1,136,6144]{2,1,0:T(8,128)(2,1)}, u32[]{:S(2)}) copy-start(bf16[1,136,6144]{2,1,0:T(8,128)(2,1)} %param.4) | copy-start | bytes 5013508
  0.6 17.0 %collective-permute-start.1 = (bf16[64,384]{1,0:T(8,128)(2,1)}, bf16[64,384]{1,0:T(8,128)(2,1)S(1)}, u32[]{:S(2)}, u32[]{:S(2)}) collective-permute-start(bf16[64,384]{1,0:T(8,128)(2,1)} %bitcast.24), channel_id=1, source_target_pairs={{0,16},{16,32},{32,48},{48,64},{64,80},{80,96},{96,112},{112,128},... | collective-permute-start | bytes 147464 | tf_op jit(solution)/shard_map/ppermute | solution.py:21
  17.6 0.8 copy-start.4
  19.4 15.5 %all-to-all-start = ((bf16[8,128,384]{2,1,0:T(8,128)(2,1)}), bf16[8,128,384]{2,1,0:T(8,128)(2,1)}, u32[]{:S(2)}, u32[]{:S(2)}) async-start(bf16[8,128,384]{2,1,0:T(8,128)(2,1)} %copies.1), calls=%async_computation | async-start | bytes 1572864 | tf_op jit(solution)/shard_map/all_to_all | solution.py:33
  25.1 7.8 %collective-permute-start = (bf16[8,136,384]{2,1,0:T(8,128)(2,1)S(1)}, bf16[8,136,384]{2,1,0:T(8,128)(2,1)S(1)}, u32[]{:S(2)}, u32[]{:S(2)}) collective-permute-start(bf16[8,136,384]{2,1,0:T(8,128)(2,1)S(1)} %get-tuple-element.11), channel_id=1, source_target_pairs={{0,1},{1,0},{2,3},{3,2},{4,5},{5,4},{6,7},{7,6},{8,9},{9,8},{10,11... | collective-permute-start | bytes 2506760 | tf_op jit(solution)/shard_map/ppermute | solution.py:25
  27.0 1.4 %copy-start.1 = (bf16[1,136,6144]{2,1,0:T(8,128)(2,1)S(1)}, bf16[1,136,6144]{2,1,0:T(8,128)(2,1)}, u32[]{:S(2)}) copy-start(bf16[1,136,6144]{2,1,0:T(8,128)(2,1)} %param.5) | copy-start | bytes 5013508
  29.5 0.9 copy-start.2
  30.4 21.2 %collective-permute-start.3 = (bf16[8,136,384]{2,1,0:T(8,128)(2,1)}, bf16[8,136,384]{2,1,0:T(8,128)(2,1)}, u32[]{:S(2)}, u32[]{:S(2)}) collective-permute-start(bf16[8,136,384]{2,1,0:T(8,128)(2,1)} %get-tuple-element.14), channel_id=1, source_target_pairs={{0,1},{1,0},{2,3},{3,2},{4,5},{5,4},{6,7},{7,6},{8,9},{9,8},{10,11... | collective-permute-start | bytes 2506760 | tf_op jit(solution)/shard_map/ppermute | solution.py:25
  42.6 9.1 %copy-start.3 = (bf16[8,136,384]{2,1,0:T(8,128)(2,1)S(1)}, bf16[8,136,384]{2,1,0:T(8,128)(2,1)}, u32[]{:S(2)}) copy-start(bf16[8,136,384]{2,1,0:T(8,128)(2,1)} %copy-done.2) | copy-start | bytes 2506756
  42.6 9.0 %collective-permute-start.2 = (bf16[2,64,256]{2,1,0:T(8,128)(2,1)S(1)}, bf16[2,64,256]{2,1,0:T(8,128)(2,1)S(1)}, u32[]{:S(2)}, u32[]{:S(2)}) collective-permute-start(bf16[2,64,256]{2,1,0:T(8,128)(2,1)S(1)} %factors_of.1.factors_ref), channel_id=1, source_target_pairs={{0,496},{16,0},{32,16},{48,32},{64,48},{80,64},{96,80},{112,96},{1... | collective-permute-start | bytes 196616 | tf_op jit(solution)/shard_map/ppermute | solution.py:21
  78.8 10.0 %collective-permute-start.4 = (f32[64,128]{1,0:T(8,128)S(1)}, f32[64,128]{1,0:T(8,128)S(1)}, u32[]{:S(2)}, u32[]{:S(2)}) collective-permute-start(f32[64,128]{1,0:T(8,128)S(1)} %add_met.1), channel_id=1, source_target_pairs={{0,16},{16,32},{32,48},{48,64},{64,80},{80,96},{96,112},{112,128},... | collective-permute-start | bytes 98312 | tf_op jit(solution)/shard_map/ppermute | solution.py:21
  100.6 8.2 %collective-permute-start.5 = (f32[64,384]{1,0:T(8,128)S(1)}, f32[64,384]{1,0:T(8,128)S(1)}, u32[]{:S(2)}, u32[]{:S(2)}) collective-permute-start(f32[64,384]{1,0:T(8,128)S(1)} %add_up.1), channel_id=1, source_target_pairs={{0,496},{16,0},{32,16},{48,32},{64,48},{80,64},{96,80},{112,96},{1... | collective-permute-start | bytes 294920 | tf_op jit(solution)/shard_map/ppermute | solution.py:21

commit v3 on v2

--- a/solution.py
+++ b/solution.py
@@ -44,19 +44,19 @@
     for k in range(0, RANK, 4):
         own, r = divmod(k, 8)
         rows = [part[own][r + i : r + i + 1, :] for i in range(4)]
-        s = [[jnp.broadcast_to(rows[i][:, k + j : k + j + 1], (1, 128)) for j in range(4)] for i in range(4)]
-        done, inv, low = list(rows), [None] * 4, {}
-        for i in range(4):
-            inv[i] = 1.0 / s[i][i]
-            for t in range(i + 1, 4):
-                low[t, i] = s[i][t] * inv[i]
-                for j in range(t, 4):
-                    s[t][j] = s[t][j] - low[t, i] * s[i][j]
-                done[t] = done[t] - low[t, i] * done[i]
-        solved = [done[i] * inv[i] for i in range(4)]
-        for i in (2, 1, 0):
-            for t in range(i + 1, 4):
-                solved[i] = solved[i] - low[t, i] * solved[t]
+        s = {(i, j): jnp.broadcast_to(rows[i][:, k + j : k + j + 1], (1, 128)) for i in range(4) for j in range(i, 4)}
+        a, b, c = s[0, 0], s[0, 1], s[1, 1]
+        first = 1.0 / (a * c - b * b)
+        e = [[(c * s[0, t] - b * s[1, t]) * first, (a * s[1, t] - b * s[0, t]) * first] for t in (2, 3)]
+        d = s[2, 2] - s[0, 2] * e[0][0] - s[1, 2] * e[0][1]
+        f = s[2, 3] - s[0, 2] * e[1][0] - s[1, 2] * e[1][1]
+        h = s[3, 3] - s[0, 3] * e[1][0] - s[1, 3] * e[1][1]
+        second = 1.0 / (d * h - f * f)
+        y = [rows[2 + t] - e[t][0] * rows[0] - e[t][1] * rows[1] for t in (0, 1)]
+        v = [(h * y[0] - f * y[1]) * second, (d * y[1] - f * y[0]) * second]
+        z = [(c * rows[0] - b * rows[1]) * first, (a * rows[1] - b * rows[0]) * first]
+        solved = [z[t] - e[0][t] * v[0] - e[1][t] * v[1] for t in (0, 1)] + v
+        done = [rows[0], rows[1] - (b / a) * rows[0], y[0], y[1] - (f / d) * y[0]]
         for g in range(own, 8):
             if g > own or r == 0:
                 less = part[g] - sum(part[g][:, k + i : k + i + 1] * solved[i] for i in range(4))
@@ -86,14 +86,14 @@
         out_ref[i, RANK:, :] = two_ref[...]
 
 
+def side_by_side(in_ref):
+    return jnp.concatenate([in_ref[i] for i in range(HALF)], axis=1)
+
+
 def half_product(core_ref, own_ref, other_ref, both_ref, out_ref):
-    core = core_ref[0]
-    own, other = jnp.zeros((ROWS, 2 * RANK), F32), jnp.zeros((ROWS, 2 * RANK), F32)
-    for i in range(HALF):
-        own += lax.dot_general(own_ref[i], both_ref[i], NT, preferred_element_type=F32)
-        other += lax.dot_general(other_ref[i], both_ref[i], NT, preferred_element_type=F32)
-    out_ref[core] = own
-    out_ref[1 - core] = other
+    core, both = core_ref[0], side_by_side(both_ref)
+    out_ref[core] = lax.dot_general(side_by_side(own_ref), both, NT, preferred_element_type=F32)
+    out_ref[1 - core] = lax.dot_general(side_by_side(other_ref), both, NT, preferred_element_type=F32)
 
 
 def factors_of(parts_ref, out_ref):
@@ -129,21 +129,22 @@
         term_ref[i] = lax.dot_general(inner, out_ref[i], TN, preferred_element_type=F32).astype(BF16)
 
 
-def residual(core_ref, micro_ref, factors_ref, error_ref):
+def residual(core_ref, micro_ref, factors_ref, error_ref, right_ref):
     left = factors_ref[core_ref[0], :, :ROWS]
     upright = left.astype(F32).T.astype(BF16)
-    for j in range(DP):
-        micro = micro_ref[:, j * SLICE : (j + 1) * SLICE]
-        right = jnp.dot(left, micro, preferred_element_type=F32).astype(BF16)
-        approx = jnp.dot(upright, right, preferred_element_type=F32)
-        error_ref[:, j * SLICE : (j + 1) * SLICE] = (micro.astype(F32) - approx).astype(BF16)
+    strips = [slice(j * SLICE, (j + 1) * SLICE) for j in range(DP)]
+    for at in strips:
+        right_ref[:, at] = jnp.dot(left, micro_ref[:, at], preferred_element_type=F32).astype(BF16)
+    for at in strips:
+        approx = jnp.dot(upright, right_ref[:, at], preferred_element_type=F32)
+        error_ref[:, at] = (micro_ref[:, at].astype(F32) - approx).astype(BF16)
 
 
 def add_up(in_ref, out_ref):
     total = in_ref[0].astype(F32)
     for i in range(1, HALF):
         total += in_ref[i].astype(F32)
-    out_ref[...] = total
+    out_ref[...] = total.astype(BF16)
 
 
 def add_and_copy(in_ref, out_ref):
@@ -165,7 +166,7 @@
 
 
 def add_met(parts_ref, out_ref):
-    out_ref[...] = parts_ref[0, :, : 2 * RANK] + parts_ref[1, :, : 2 * RANK]
+    out_ref[...] = (parts_ref[0, :, : 2 * RANK] + parts_ref[1, :, : 2 * RANK]).astype(BF16)
 
 
 def factor(parts_ref, out_ref):
@@ -174,28 +175,29 @@
 
 
 def expand(met_ref, right_ref, out_ref):
-    met = met_ref[...].astype(BF16)
+    met = met_ref[...]
     for i in range(HALF):
         out_ref[i] = jnp.dot(met, right_ref[i], preferred_element_type=F32).astype(BF16)
 
 
 def finish(inverse_ref, in_ref, out_ref):
-    out_ref[...] = jnp.dot(inverse_ref[...], in_ref[...], precision=HIGH, preferred_element_type=F32)
+    out_ref[...] = jnp.dot(inverse_ref[...], in_ref[...].astype(F32), precision=HIGH, preferred_element_type=F32)
 
 
 VMEM = pl.BlockSpec(memory_space=pltpu.VMEM)
 SMEM = pl.BlockSpec(memory_space=pltpu.SMEM)
 
 
-def kernel(body, *shapes, flops=0):
+def kernel(body, *shapes, flops=0, scratch=()):
     outs = [jax.ShapeDtypeStruct(shape, dtype) for shape, dtype in shapes]
-    names = body.__code__.co_varnames[: body.__code__.co_argcount - len(outs)]
+    names = body.__code__.co_varnames[: body.__code__.co_argcount - len(outs) - len(scratch)]
     return pl.pallas_call(
         body,
         out_shape=outs if len(outs) > 1 else outs[0],
         in_specs=[SMEM if name == "core_ref" else VMEM for name in names],
-        compiler_params=pltpu.CompilerParams(vmem_limit_bytes=32 * 2**20),
+        compiler_params=pltpu.CompilerParams(vmem_limit_bytes=10 * 2**20),
         cost_estimate=pl.CostEstimate(flops=flops, bytes_accessed=2**20, transcendentals=0),
+        scratch_shapes=list(scratch),
         name=body.__name__,
     )
 
@@ -217,15 +219,15 @@
     part = kernel(half_product, ((2, ROWS, 2 * RANK), F32), flops=2 * product)(core, micro_own, micro_other, both)
     factors = kernel(factors_of, ((2, RANK, 256), BF16), flops=4 * product)(both_cores(part))
     factors_in = passed_along(factors, -1)
-    error = kernel(residual, ((ROWS, D), BF16), flops=2 * product)(core, micro, factors)
+    error = kernel(residual, ((ROWS, D), BF16), flops=2 * product, scratch=[pltpu.VMEM((RANK, D), BF16)])(core, micro, factors)
     factors_in, error = lax.optimization_barrier((factors_in, error))
     right = kernel(against, stacked, flops=product)(core, micro_own, micro_other, factors)
     terms, summed = kernel(project, stacked, blocks, flops=product)(core, rows_own, rows_other, factors_in)
     whole = across(kernel(add_and_copy, blocks)(across(summed)))
     met = both_cores(kernel(meet, ((RANK, 256), F32), flops=product)(whole, terms))
-    met_in = passed_along(kernel(add_met, ((RANK, 2 * RANK), F32))(met), 1)
+    met_in = passed_along(kernel(add_met, ((RANK, 2 * RANK), BF16))(met), 1)
     parts = across(kernel(expand, blocks, flops=product)(met_in, right))
-    parts = passed_along(kernel(add_up, ((RANK, SLICE), F32))(parts), -1)
+    parts = passed_along(kernel(add_up, ((RANK, SLICE), BF16))(parts), -1)
     inverse = kernel(factor, ((RANK, RANK), F32), flops=4 * product)(met)
     weight_right = kernel(finish, ((RANK, SLICE), F32))(inverse, parts)
     return error[None], weight_right.T[None]

time: 110 us -> 107 us (0.973)
  the two profiles are of different devices: /device:TPU:2 before, /device:TPU:1 now
where the time goes in v3:
time: 107 us; the launch traced here: 105 us
  blocking collectives  39.1 us (37%)
  starting transfers between devices  27 us (25%)
  waiting for transfers between devices  18.7 us (17%)
  Pallas kernels  16.3 us (15%)
  local copies, waits for them, and re-layouts  3.17 us (3%)
    all_to_all x3, blocking collectives, across(): lax.all_to_all(blocks, 'dp', 0, 0, tiled=True, axis_index_groups=ACROSS)  29.5 us
    ppermute x4, waiting for transfers between devices, passed_along(): lax.ppermute(shard, 'pipe', [(i, (i + by) % devices) for i in range(devic...  16.9 us
    ppermute x4, starting transfers between devices, passed_along(): lax.ppermute(shard, 'pipe', [(i, (i + by) % devices) for i in range(devic...  16.4 us
    all_gather x2, blocking collectives, both_cores(): return lax.all_gather(shard, 'dp', axis_index_groups=CORES)  9.56 us
    ppermute x2, starting transfers between devices, exchanged(): return lax.ppermute(shard, 'dp', [(i, i ^ 1) for i in range(DP)])  5.77 us
    all_to_all x1, starting transfers between devices, across(): lax.all_to_all(blocks, 'dp', 0, 0, tiled=True, axis_index_groups=ACROSS)  4.81 us
    pallas_call x1, Pallas kernels, local(): kernel(factors_of, ((2, RANK, 256), BF16), flops=4 * product)  3.59 us
    unnamed x10, local copies, waits for them, and re-layouts  3.17 us
  transfers between devices with their start and end apart: 7, of which 4 were waited for; matrix products, arithmetic and copies ran while one was open for 0% of the time, Pallas kernels for 11%

profile of v3, /device:TPU:1, one launch (start us, length us, event | category | flops | bytes accessed | tf_op | source)
XLA Modules:
  0.0 105.1 jit_solution(7286168030429620272)
XLA Ops:
  0.6 6.8 %collective-permute-start.1 = (bf16[64,384]{1,0:T(8,128)(2,1)}, bf16[64,384]{1,0:T(8,128)(2,1)S(1)}, u32[]{:S(2)}, u32[]{:S(2)}) collective-permute-start(bf16[64,384]{1,0:T(8,128)(2,1)} %bitcast.24), channel_id=1, source_target_pairs={{0,16},{16,32},{32,48},{48,64},{64,80},{80,96},{96,112},{112,128},... | collective-permute-start | bytes 147464 | tf_op jit(solution)/shard_map/ppermute | solution.py:21
  7.4 10.0 %collective-permute-done.1.two_ref = bf16[64,384]{1,0:T(8,128)(2,1)S(1)} collective-permute-done((bf16[64,384]{1,0:T(8,128)(2,1)}, bf16[64,384]{1,0:T(8,128)(2,1)S(1)}, u32[]{:S(2)}, u32[]{:S(2)}) %collective-permute-start.1) | collective-permute-done | bytes 49184 | tf_op jit(solution)/shard_map/ppermute | solution.py:21
  18.2 0.9 copies.1
  19.1 4.8 %all-to-all-start = ((bf16[8,128,384]{2,1,0:T(8,128)(2,1)}), bf16[8,128,384]{2,1,0:T(8,128)(2,1)}, u32[]{:S(2)}, u32[]{:S(2)}) async-start(bf16[8,128,384]{2,1,0:T(8,128)(2,1)} %copies.1), calls=%async_computation | async-start | bytes 1572864 | tf_op jit(solution)/shard_map/all_to_all | solution.py:33
  24.1 3.9 %collective-permute-start = (bf16[8,136,384]{2,1,0:T(8,128)(2,1)S(1)}, bf16[8,136,384]{2,1,0:T(8,128)(2,1)S(1)}, u32[]{:S(2)}, u32[]{:S(2)}) collective-permute-start(bf16[8,136,384]{2,1,0:T(8,128)(2,1)S(1)} %get-tuple-element.11), channel_id=1, source_target_pairs={{0,1},{1,0},{2,3},{3,2},{4,5},{5,4},{6,7},{7,6},{8,9},{9,8},{10,11... | collective-permute-start | bytes 2506760 | tf_op jit(solution)/shard_map/ppermute | solution.py:25
  28.0 1.4 %copy-done.1 = bf16[1,136,6144]{2,1,0:T(8,128)(2,1)S(1)} copy-done((bf16[1,136,6144]{2,1,0:T(8,128)(2,1)S(1)}, bf16[1,136,6144]{2,1,0:T(8,128)(2,1)}, u32[]{:S(2)}) %copy-start.1) | copy-done | bytes 1671192
  29.4 1.1 %split_halves.3 = (bf16[8,136,384]{2,1,0:T(8,128)(2,1)S(1)}, bf16[8,136,384]{2,1,0:T(8,128)(2,1)}) custom-call(s32[1]{0:T(128)} %bitcast.core_ref, bf16[136,6144]{1,0:T(8,128)(2,1)S(1)} %bitcast.17), custom_call_target="tpu_custom_call" | custom-call | bytes 1048576 | tf_op jit(solution)/shard_map/split_halves/pallas_call | solution.py:217
  30.5 0.9 copy-done.2
  31.4 1.9 %collective-permute-start.3 = (bf16[8,136,384]{2,1,0:T(8,128)(2,1)}, bf16[8,136,384]{2,1,0:T(8,128)(2,1)}, u32[]{:S(2)}, u32[]{:S(2)}) collective-permute-start(bf16[8,136,384]{2,1,0:T(8,128)(2,1)} %get-tuple-element.14), channel_id=1, source_target_pairs={{0,1},{1,0},{2,3},{3,2},{4,5},{5,4},{6,7},{7,6},{8,9},{9,8},{10,11... | collective-permute-start | bytes 2506760 | tf_op jit(solution)/shard_map/ppermute | solution.py:25
  33.4 1.7 %all-to-all-done.both_ref = bf16[8,128,384]{2,1,0:T(8,128)(2,1)} async-done(((bf16[8,128,384]{2,1,0:T(8,128)(2,1)}), bf16[8,128,384]{2,1,0:T(8,128)(2,1)}, u32[]{:S(2)}, u32[]{:S(2)}) %all-to-all-start) | async-done | bytes 786464 | tf_op jit(solution)/shard_map/all_to_all | solution.py:33
  35.1 1.8 %half_product.1 = f32[2,136,128]{2,1,0:T(8,128)S(1)} custom-call(s32[1]{0:T(128)} %bitcast.core_ref, bf16[8,136,384]{2,1,0:T(8,128)(2,1)S(1)} %get-tuple-element.10.own_ref, bf16[8,136,384]{2,1,0:T(8,128)(2,1)S(1)} %collective-permute-done.other_ref, bf16[8,128,384]{2,1,0:T(8,128)(2,1)} %all-to-all-done.both_ref), custom_call_target="tpu_custom_call" | custom-call | flops 213909504 | bytes 1048576 | tf_op jit(solution)/shard_map/half_product/pallas_call | solution.py:219
  36.9 4.5 %all-gather = f32[4,136,128]{2,1,0:T(8,128)S(1)} all-gather(f32[2,136,128]{2,1,0:T(8,128)S(1)} %half_product.1), channel_id=2, replica_groups={{0,1},{2,3},{4,5},{6,7},{8,9},{10,11},{12,13},{14,15},{16,17},{18,19},{..., dimensions={0}, use_global_device_ids=true | all-gather | bytes 417792 | tf_op jit(solution)/shard_map/all_gather | solution.py:29
  41.4 3.6 %factors_of.1.factors_ref = bf16[2,64,256]{2,1,0:T(8,128)(2,1)S(1)} custom-call(f32[2,2,136,128]{3,2,1,0:T(8,128)S(1)} %bitcast.20), custom_call_target="tpu_custom_call" | custom-call | flops 427819008 | bytes 1048576 | tf_op jit(solution)/shard_map/factors_of/pallas_call | solution.py:220
  45.0 4.5 %collective-permute-start.2 = (bf16[2,64,256]{2,1,0:T(8,128)(2,1)S(1)}, bf16[2,64,256]{2,1,0:T(8,128)(2,1)S(1)}, u32[]{:S(2)}, u32[]{:S(2)}) collective-permute-start(bf16[2,64,256]{2,1,0:T(8,128)(2,1)S(1)} %factors_of.1.factors_ref), channel_id=1, source_target_pairs={{0,496},{16,0},{32,16},{48,32},{64,48},{80,64},{96,80},{112,96},{1... | collective-permute-start | bytes 196616 | tf_op jit(solution)/shard_map/ppermute | solution.py:21
  49.5 2.3 %residual.1 = bf16[136,6144]{1,0:T(8,128)(2,1)} custom-call(s32[1]{0:T(128)} %bitcast.core_ref, bf16[136,6144]{1,0:T(8,128)(2,1)S(1)} %bitcast.16, bf16[2,64,256]{2,1,0:T(8,128)(2,1)S(1)} %factors_of.1.factors_ref), custom_call_target="tpu_custom_call" | custom-call | flops 213909504 | bytes 1048576 | tf_op jit(solution)/shard_map/residual/pallas_call | solution.py:222
  51.7 1.9 %project.1 = (bf16[8,128,384]{2,1,0:T(8,128)(2,1)S(1)}, bf16[8,64,384]{2,1,0:T(8,128)(2,1)S(1)}) custom-call(s32[1]{0:T(128)} %bitcast.core_ref, bf16[8,136,384]{2,1,0:T(8,128)(2,1)S(1)} %copy-done.3, bf16[8,136,384]{2,1,0:T(8,128)(2,1)} %collective-permute-done.3.other_ref, bf16[2,64,256]{2,1,0:T(8,128)(2,1)S(1)} %collective-permute-done.2.factors_ref), custom_call_target="tpu_custom_call" | custom-call | flops 106954752 | bytes 1048576 | tf_op jit(solution)/shard_map/project/pallas_call | solution.py:225
  53.6 10.4 %all_to_all.20.in_ref = bf16[8,64,384]{2,1,0:T(8,128)(2,1)S(1)} all-to-all(bf16[8,64,384]{2,1,0:T(8,128)(2,1)S(1)} %get-tuple-element.16), channel_id=1, replica_groups={{0,2,4,6,8,10,12,14},{1,3,5,7,9,11,13,15},{16,18,20,22,24,26,28,30},{17..., dimensions={0} | all-to-all | bytes 786432 | tf_op jit(solution)/shard_map/all_to_all | solution.py:33
  64.1 9.5 %all_to_all.21.whole_ref = bf16[8,64,384]{2,1,0:T(8,128)(2,1)S(1)} all-to-all(bf16[8,64,384]{2,1,0:T(8,128)(2,1)S(1)} %add_and_copy.1), channel_id=1, replica_groups={{0,2,4,6,8,10,12,14},{1,3,5,7,9,11,13,15},{16,18,20,22,24,26,28,30},{17..., dimensions={0} | all-to-all | bytes 786432 | tf_op jit(solution)/shard_map/all_to_all | solution.py:33
  74.2 5.1 %all-gather.1 = f32[128,256]{1,0:T(8,128)S(1)} all-gather(f32[64,256]{1,0:T(8,128)S(1)} %meet.1), channel_id=3, replica_groups={{0,1},{2,3},{4,5},{6,7},{8,9},{10,11},{12,13},{14,15},{16,17},{18,19},{..., dimensions={0}, use_global_device_ids=true | all-gather | bytes 196608 | tf_op jit(solution)/shard_map/all_gather | solution.py:29
  79.3 1.9 %collective-permute-start.4 = (bf16[64,128]{1,0:T(8,128)(2,1)S(1)}, bf16[64,128]{1,0:T(8,128)(2,1)S(1)}, u32[]{:S(2)}, u32[]{:S(2)}) collective-permute-start(bf16[64,128]{1,0:T(8,128)(2,1)S(1)} %add_met.1), channel_id=1, source_target_pairs={{0,16},{16,32},{32,48},{48,64},{64,80},{80,96},{96,112},{112,128},... | collective-permute-start | bytes 49160 | tf_op jit(solution)/shard_map/ppermute | solution.py:21
  81.7 6.4 %collective-permute-done.4.met_ref = bf16[64,128]{1,0:T(8,128)(2,1)S(1)} collective-permute-done((bf16[64,128]{1,0:T(8,128)(2,1)S(1)}, bf16[64,128]{1,0:T(8,128)(2,1)S(1)}, u32[]{:S(2)}, u32[]{:S(2)}) %collective-permute-start.4) | collective-permute-done | bytes 16416 | tf_op jit(solution)/shard_map/ppermute | solution.py:21
  88.3 9.7 %all_to_all.22.in_ref = bf16[8,64,384]{2,1,0:T(8,128)(2,1)S(1)} all-to-all(bf16[8,64,384]{2,1,0:T(8,128)(2,1)S(1)} %expand.1), channel_id=1, replica_groups={{0,2,4,6,8,10,12,14},{1,3,5,7,9,11,13,15},{16,18,20,22,24,26,28,30},{17..., dimensions={0} | all-to-all | bytes 786432 | tf_op jit(solution)/shard_map/all_to_all | solution.py:33
  98.0 3.3 %collective-permute-start.5 = (bf16[64,384]{1,0:T(8,128)(2,1)S(1)}, bf16[64,384]{1,0:T(8,128)(2,1)S(1)}, u32[]{:S(2)}, u32[]{:S(2)}) collective-permute-start(bf16[64,384]{1,0:T(8,128)(2,1)S(1)} %add_up.1), channel_id=1, source_target_pairs={{0,496},{16,0},{32,16},{48,32},{64,48},{80,64},{96,80},{112,96},{1... | collective-permute-start | bytes 147464 | tf_op jit(solution)/shard_map/ppermute | solution.py:21
  101.3 2.3 %factor.1.inverse_ref = f32[64,64]{1,0:T(8,128)S(1)} custom-call(f32[2,64,256]{2,1,0:T(8,128)S(1)} %bitcast.19), custom_call_target="tpu_custom_call" | custom-call | flops 427819008 | bytes 1048576 | tf_op jit(solution)/shard_map/factor/pallas_call | solution.py:231
  (20 shorter events, 3.9 us)
Async XLA Ops:
  0.6 23.3 %copy-start = (bf16[1,136,6144]{2,1,0:T(8,128)(2,1)S(1)}, bf16[1,136,6144]{2,1,0:T(8,128)(2,1)}, u32[]{:S(2)}) copy-start(bf16[1,136,6144]{2,1,0:T(8,128)(2,1)} %param.4) | copy-start | bytes 5013508
  0.6 16.7 %collective-permute-start.1 = (bf16[64,384]{1,0:T(8,128)(2,1)}, bf16[64,384]{1,0:T(8,128)(2,1)S(1)}, u32[]{:S(2)}, u32[]{:S(2)}) collective-permute-start(bf16[64,384]{1,0:T(8,128)(2,1)} %bitcast.24), channel_id=1, source_target_pairs={{0,16},{16,32},{32,48},{48,64},{64,80},{80,96},{96,112},{112,128},... | collective-permute-start | bytes 147464 | tf_op jit(solution)/shard_map/ppermute | solution.py:21
  17.4 0.8 copy-start.4
  19.1 16.0 %all-to-all-start = ((bf16[8,128,384]{2,1,0:T(8,128)(2,1)}), bf16[8,128,384]{2,1,0:T(8,128)(2,1)}, u32[]{:S(2)}, u32[]{:S(2)}) async-start(bf16[8,128,384]{2,1,0:T(8,128)(2,1)} %copies.1), calls=%async_computation | async-start | bytes 1572864 | tf_op jit(solution)/shard_map/all_to_all | solution.py:33
  24.1 9.2 %collective-permute-start = (bf16[8,136,384]{2,1,0:T(8,128)(2,1)S(1)}, bf16[8,136,384]{2,1,0:T(8,128)(2,1)S(1)}, u32[]{:S(2)}, u32[]{:S(2)}) collective-permute-start(bf16[8,136,384]{2,1,0:T(8,128)(2,1)S(1)} %get-tuple-element.11), channel_id=1, source_target_pairs={{0,1},{1,0},{2,3},{3,2},{4,5},{5,4},{6,7},{7,6},{8,9},{9,8},{10,11... | collective-permute-start | bytes 2506760 | tf_op jit(solution)/shard_map/ppermute | solution.py:25
  28.0 1.4 %copy-start.1 = (bf16[1,136,6144]{2,1,0:T(8,128)(2,1)S(1)}, bf16[1,136,6144]{2,1,0:T(8,128)(2,1)}, u32[]{:S(2)}) copy-start(bf16[1,136,6144]{2,1,0:T(8,128)(2,1)} %param.5) | copy-start | bytes 5013508
  30.5 0.9 copy-start.2
  31.4 20.3 %collective-permute-start.3 = (bf16[8,136,384]{2,1,0:T(8,128)(2,1)}, bf16[8,136,384]{2,1,0:T(8,128)(2,1)}, u32[]{:S(2)}, u32[]{:S(2)}) collective-permute-start(bf16[8,136,384]{2,1,0:T(8,128)(2,1)} %get-tuple-element.14), channel_id=1, source_target_pairs={{0,1},{1,0},{2,3},{3,2},{4,5},{5,4},{6,7},{7,6},{8,9},{9,8},{10,11... | collective-permute-start | bytes 2506760 | tf_op jit(solution)/shard_map/ppermute | solution.py:25
  45.0 6.8 %copy-start.3 = (bf16[8,136,384]{2,1,0:T(8,128)(2,1)S(1)}, bf16[8,136,384]{2,1,0:T(8,128)(2,1)}, u32[]{:S(2)}) copy-start(bf16[8,136,384]{2,1,0:T(8,128)(2,1)} %copy-done.2) | copy-start | bytes 2506756
  45.0 6.8 %collective-permute-start.2 = (bf16[2,64,256]{2,1,0:T(8,128)(2,1)S(1)}, bf16[2,64,256]{2,1,0:T(8,128)(2,1)S(1)}, u32[]{:S(2)}, u32[]{:S(2)}) collective-permute-start(bf16[2,64,256]{2,1,0:T(8,128)(2,1)S(1)} %factors_of.1.factors_ref), channel_id=1, source_target_pairs={{0,496},{16,0},{32,16},{48,32},{64,48},{80,64},{96,80},{112,96},{1... | collective-permute-start | bytes 196616 | tf_op jit(solution)/shard_map/ppermute | solution.py:21
  79.3 8.8 %collective-permute-start.4 = (bf16[64,128]{1,0:T(8,128)(2,1)S(1)}, bf16[64,128]{1,0:T(8,128)(2,1)S(1)}, u32[]{:S(2)}, u32[]{:S(2)}) collective-permute-start(bf16[64,128]{1,0:T(8,128)(2,1)S(1)} %add_met.1), channel_id=1, source_target_pairs={{0,16},{16,32},{32,48},{48,64},{64,80},{80,96},{96,112},{112,128},... | collective-permute-start | bytes 49160 | tf_op jit(solution)/shard_map/ppermute | solution.py:21
  98.0 6.1 %collective-permute-start.5 = (bf16[64,384]{1,0:T(8,128)(2,1)S(1)}, bf16[64,384]{1,0:T(8,128)(2,1)S(1)}, u32[]{:S(2)}, u32[]{:S(2)}) collective-permute-start(bf16[64,384]{1,0:T(8,128)(2,1)S(1)} %add_up.1), channel_id=1, source_target_pairs={{0,496},{16,0},{32,16},{48,32},{64,48},{80,64},{96,80},{112,96},{1... | collective-permute-start | bytes 147464 | tf_op jit(solution)/shard_map/ppermute | solution.py:21

commit v4 on v3

--- a/solution.py
+++ b/solution.py
@@ -101,14 +101,10 @@
     raw = [both[:RANK] for both in total]
     gram = [lax.dot_general(a, a, NT, precision=HIGH, preferred_element_type=F32) for a in raw]
     inverse = [inverse_cholesky(a) for a in gram]
+    warm = [lax.dot_general(both[:RANK], both[RANK:], NT, precision=HIGH, preferred_element_type=F32) for both in total]
     for slot in range(2):
-        left = jnp.dot(inverse[slot], raw[slot], precision=HIGH, preferred_element_type=F32).astype(BF16)
-        inner = lax.dot_general(
-            left.astype(F32), total[slot][RANK:], NT, precision=HIGH, preferred_element_type=F32
-        )
-        out_ref[slot] = jnp.zeros((RANK, 256), BF16)
-        out_ref[slot, :, :ROWS] = left
-        out_ref[slot, :, 192:] = inner.astype(BF16)
+        both = jnp.concatenate([raw[slot], jnp.zeros((RANK, 192 - ROWS), F32), warm[slot]], axis=1)
+        out_ref[slot] = jnp.dot(inverse[slot], both, precision=HIGH, preferred_element_type=F32).astype(BF16)
 
 
 def against(core_ref, own_ref, other_ref, factors_ref, out_ref):
@@ -156,12 +152,9 @@
 
 
 def meet(whole_ref, terms_ref, out_ref):
-    met, gram = jnp.zeros((RANK, 2 * RANK), F32), jnp.zeros((RANK, RANK), F32)
-    for i in range(HALF):
-        met += lax.dot_general(whole_ref[i], terms_ref[i], NT, preferred_element_type=F32)
-        gram += lax.dot_general(whole_ref[i], whole_ref[i], NT, preferred_element_type=F32)
-    out_ref[:, : 2 * RANK] = met
-    out_ref[:, 2 * RANK : 3 * RANK] = gram
+    whole = side_by_side(whole_ref)
+    out_ref[:, : 2 * RANK] = lax.dot_general(whole, side_by_side(terms_ref), NT, preferred_element_type=F32)
+    out_ref[:, 2 * RANK : 3 * RANK] = lax.dot_general(whole, whole, NT, preferred_element_type=F32)
     out_ref[:, 3 * RANK :] = jnp.zeros((RANK, RANK), F32)
 
 
@@ -184,11 +177,12 @@
     out_ref[...] = jnp.dot(inverse_ref[...], in_ref[...].astype(F32), precision=HIGH, preferred_element_type=F32)
 
 
+LONG = 2**36
 VMEM = pl.BlockSpec(memory_space=pltpu.VMEM)
 SMEM = pl.BlockSpec(memory_space=pltpu.SMEM)
 
 
-def kernel(body, *shapes, flops=0, scratch=()):
+def kernel(body, *shapes, flops=0, moved=2**20, scratch=()):
     outs = [jax.ShapeDtypeStruct(shape, dtype) for shape, dtype in shapes]
     names = body.__code__.co_varnames[: body.__code__.co_argcount - len(outs) - len(scratch)]
     return pl.pallas_call(
@@ -196,7 +190,7 @@
         out_shape=outs if len(outs) > 1 else outs[0],
         in_specs=[SMEM if name == "core_ref" else VMEM for name in names],
         compiler_params=pltpu.CompilerParams(vmem_limit_bytes=10 * 2**20),
-        cost_estimate=pl.CostEstimate(flops=flops, bytes_accessed=2**20, transcendentals=0),
+        cost_estimate=pl.CostEstimate(flops=flops, bytes_accessed=moved, transcendentals=0),
         scratch_shapes=list(scratch),
         name=body.__name__,
     )
@@ -211,21 +205,26 @@
     blocks = ((HALF, RANK, SLICE), BF16)
 
     warm = passed_along(weight_basis[0].T, 1)
-    both = across(kernel(copies, stacked)(act_basis[0].T, warm))
     micro_own, micro_other = kernel(split_halves, halves, halves)(core, micro)
     micro_other = exchanged(micro_other)
-    rows_own, rows_other = kernel(split_halves, halves, halves)(core, rows)
-    rows_other = exchanged(rows_other)
+    both = kernel(copies, stacked, flops=LONG)(act_basis[0].T, warm)
+    both, micro_other = lax.optimization_barrier((both, micro_other))
+    both = across(both)
     part = kernel(half_product, ((2, ROWS, 2 * RANK), F32), flops=2 * product)(core, micro_own, micro_other, both)
     factors = kernel(factors_of, ((2, RANK, 256), BF16), flops=4 * product)(both_cores(part))
     factors_in = passed_along(factors, -1)
-    error = kernel(residual, ((ROWS, D), BF16), flops=2 * product, scratch=[pltpu.VMEM((RANK, D), BF16)])(core, micro, factors)
-    factors_in, error = lax.optimization_barrier((factors_in, error))
-    right = kernel(against, stacked, flops=product)(core, micro_own, micro_other, factors)
+    rows_own, rows_other = kernel(split_halves, halves, halves)(core, lax.optimization_barrier((rows, factors))[0])
+    rows_other = exchanged(rows_other)
+    right = kernel(against, stacked, flops=LONG)(core, micro_own, micro_other, factors)
+    error = kernel(residual, ((ROWS, D), BF16), flops=2 * product, scratch=[pltpu.VMEM((RANK, D), BF16)])(
+        core, micro, factors
+    )
+    factors_in, rows_other, right = lax.optimization_barrier((factors_in, rows_other, right))
     terms, summed = kernel(project, stacked, blocks, flops=product)(core, rows_own, rows_other, factors_in)
     whole = across(kernel(add_and_copy, blocks)(across(summed)))
     met = both_cores(kernel(meet, ((RANK, 256), F32), flops=product)(whole, terms))
     met_in = passed_along(kernel(add_met, ((RANK, 2 * RANK), BF16))(met), 1)
+    met_in, error = lax.optimization_barrier((met_in, error))
     parts = across(kernel(expand, blocks, flops=product)(met_in, right))
     parts = passed_along(kernel(add_up, ((RANK, SLICE), BF16))(parts), -1)
     inverse = kernel(factor, ((RANK, RANK), F32), flops=4 * product)(met)

time: 107 us -> 105 us (0.981)
  blocking collectives: 39.1 us -> 54.2 us
  waiting for transfers between devices: 18.7 us -> 10.4 us
  Pallas kernels: 16.3 us -> 11.7 us
  starting transfers between devices: 27 us -> 24.9 us
  local copies, waits for them, and re-layouts: 3.17 us -> 1.45 us
    all_to_all x3 -> x4, blocking collectives: 29.5 us -> 45.9 us  [across(): lax.all_to_all(blocks, 'dp', 0, 0, tiled=True, axis_index_groups=ACROSS)]
    ppermute x4, waiting for transfers between devices: 16.9 us -> 8.96 us  [passed_along(): lax.ppermute(shard, 'pipe', [(i, (i + by) % devices) for i in range(devic...]
    all_to_all x1 -> x0, starting transfers between devices: 4.81 us -> none  [across(): lax.all_to_all(blocks, 'dp', 0, 0, tiled=True, axis_index_groups=ACROSS)]
    ppermute x4, starting transfers between devices: 16.4 us -> 18.3 us  [passed_along(): lax.ppermute(shard, 'pipe', [(i, (i + by) % devices) for i in range(devic...]
    pallas_call x3, Pallas kernels: 2.48 us -> 0.69 us  [the longest x1 0.46 us: local(): kernel(against, stacked, flops=LONG)(core, micro_own, micro_other, factors)]
    all_to_all x1 -> x0, waiting for transfers between devices: 1.74 us -> none  [across(): lax.all_to_all(blocks, 'dp', 0, 0, tiled=True, axis_index_groups=ACROSS)]
    unnamed x10 -> x8, local copies, waits for them, and re-layouts: 3.17 us -> 1.45 us
    ppermute x2, waiting for transfers between devices: 0.01 us -> 1.48 us  [exchanged(): return lax.ppermute(shard, 'dp', [(i, i ^ 1) for i in range(DP)])]
  transfers between devices with their start and end apart: 7 -> 6, of which waited for: 4 -> 4; matrix products, arithmetic and copies ran while one was open for 0% -> 0% of each run, Pallas kernels for 11% -> 5%
where the time goes in v4:
time: 105 us; the launch traced here: 104 us
  blocking collectives  54.2 us (52%)
  starting transfers between devices  24.9 us (24%)
  Pallas kernels  11.7 us (11%)
  waiting for transfers between devices  10.4 us (10%)
  local copies, waits for them, and re-layouts  1.45 us (1%)
    all_to_all x4, blocking collectives, across(): lax.all_to_all(blocks, 'dp', 0, 0, tiled=True, axis_index_groups=ACROSS)  45.9 us
    ppermute x4, starting transfers between devices, passed_along(): lax.ppermute(shard, 'pipe', [(i, (i + by) % devices) for i in range(devic...  18.3 us
    ppermute x4, waiting for transfers between devices, passed_along(): lax.ppermute(shard, 'pipe', [(i, (i + by) % devices) for i in range(devic...  8.96 us
    all_gather x2, blocking collectives, both_cores(): return lax.all_gather(shard, 'dp', axis_index_groups=CORES)  8.32 us
    ppermute x2, starting transfers between devices, exchanged(): return lax.ppermute(shard, 'dp', [(i, i ^ 1) for i in range(DP)])  6.6 us
    pallas_call x1, Pallas kernels, local(): kernel(factors_of, ((2, RANK, 256), BF16), flops=4 * product)  3.16 us
    pallas_call x1, Pallas kernels, local(): inverse = kernel(factor, ((RANK, RANK), F32), flops=4 * product)(met)  2.29 us
    pallas_call x1, Pallas kernels, local(): kernel(residual, ((ROWS, D), BF16), flops=2 * product, scratch=[pltpu.VME...  2.26 us
  transfers between devices with their start and end apart: 6, of which 4 were waited for; matrix products, arithmetic and copies ran while one was open for 0% of the time, Pallas kernels for 5%

profile of v4, /device:TPU:1, one launch (start us, length us, event | category | flops | bytes accessed | tf_op | source)
XLA Modules:
  0.0 103.5 jit_solution(14752708550958005460)
XLA Ops:
  0.6 6.6 %collective-permute-start = (bf16[64,384]{1,0:T(8,128)(2,1)}, bf16[64,384]{1,0:T(8,128)(2,1)S(1)}, u32[]{:S(2)}, u32[]{:S(2)}) collective-permute-start(bf16[64,384]{1,0:T(8,128)(2,1)} %bitcast.24), channel_id=1, source_target_pairs={{0,16},{16,32},{32,48},{48,64},{64,80},{80,96},{96,112},{112,128},... | collective-permute-start | bytes 147464 | tf_op jit(solution)/shard_map/ppermute | solution.py:21
  7.3 1.4 %copy-done = bf16[1,136,6144]{2,1,0:T(8,128)(2,1)S(1)} copy-done((bf16[1,136,6144]{2,1,0:T(8,128)(2,1)S(1)}, bf16[1,136,6144]{2,1,0:T(8,128)(2,1)}, u32[]{:S(2)}) %copy-start) | copy-done | bytes 1671192
  8.9 4.1 %collective-permute-start.1 = (bf16[8,136,384]{2,1,0:T(8,128)(2,1)S(1)}, bf16[8,136,384]{2,1,0:T(8,128)(2,1)S(1)}, u32[]{:S(2)}, u32[]{:S(2)}) collective-permute-start(bf16[8,136,384]{2,1,0:T(8,128)(2,1)S(1)} %get-tuple-element.17), channel_id=1, source_target_pairs={{0,1},{1,0},{2,3},{3,2},{4,5},{5,4},{6,7},{7,6},{8,9},{9,8},{10,11... | collective-permute-start | bytes 2506760 | tf_op jit(solution)/shard_map/ppermute | solution.py:25
  13.0 4.3 %collective-permute-done.two_ref = bf16[64,384]{1,0:T(8,128)(2,1)S(1)} collective-permute-done((bf16[64,384]{1,0:T(8,128)(2,1)}, bf16[64,384]{1,0:T(8,128)(2,1)S(1)}, u32[]{:S(2)}, u32[]{:S(2)}) %collective-permute-start) | collective-permute-done | bytes 49184 | tf_op jit(solution)/shard_map/ppermute | solution.py:21
  17.3 15.6 %all_to_all.20.both_ref = bf16[8,128,384]{2,1,0:T(8,128)(2,1)S(1)} all-to-all(bf16[8,128,384]{2,1,0:T(8,128)(2,1)S(1)} %copies.1), channel_id=1, replica_groups={{0,2,4,6,8,10,12,14},{1,3,5,7,9,11,13,15},{16,18,20,22,24,26,28,30},{17..., dimensions={0} | all-to-all | bytes 1572864 | tf_op jit(solution)/shard_map/all_to_all | solution.py:33
  32.9 0.6 half_product.1
  33.5 4.5 %all-gather = f32[4,136,128]{2,1,0:T(8,128)S(1)} all-gather(f32[2,136,128]{2,1,0:T(8,128)S(1)} %half_product.1), channel_id=2, replica_groups={{0,1},{2,3},{4,5},{6,7},{8,9},{10,11},{12,13},{14,15},{16,17},{18,19},{..., dimensions={0}, use_global_device_ids=true | all-gather | bytes 417792 | tf_op jit(solution)/shard_map/all_gather | solution.py:29
  38.0 3.2 %factors_of.1.factors_ref = bf16[2,64,256]{2,1,0:T(8,128)(2,1)S(1)} custom-call(f32[2,2,136,128]{3,2,1,0:T(8,128)S(1)} %bitcast.20), custom_call_target="tpu_custom_call" | custom-call | flops 427819008 | bytes 1048576 | tf_op jit(solution)/shard_map/factors_of/pallas_call | solution.py:214
  41.2 5.9 %collective-permute-start.2 = (bf16[2,64,256]{2,1,0:T(8,128)(2,1)S(1)}, bf16[2,64,256]{2,1,0:T(8,128)(2,1)S(1)}, u32[]{:S(2)}, u32[]{:S(2)}) collective-permute-start(bf16[2,64,256]{2,1,0:T(8,128)(2,1)S(1)} %factors_of.1.factors_ref), channel_id=1, source_target_pairs={{0,496},{16,0},{32,16},{48,32},{64,48},{80,64},{96,80},{112,96},{1... | collective-permute-start | bytes 196616 | tf_op jit(solution)/shard_map/ppermute | solution.py:21
  47.3 2.5 %collective-permute-start.3 = (bf16[8,136,384]{2,1,0:T(8,128)(2,1)S(1)}, bf16[8,136,384]{2,1,0:T(8,128)(2,1)S(1)}, u32[]{:S(2)}, u32[]{:S(2)}) collective-permute-start(bf16[8,136,384]{2,1,0:T(8,128)(2,1)S(1)} %get-tuple-element.22), channel_id=1, source_target_pairs={{0,1},{1,0},{2,3},{3,2},{4,5},{5,4},{6,7},{7,6},{8,9},{9,8},{10,11... | collective-permute-start | bytes 2506760 | tf_op jit(solution)/shard_map/ppermute | solution.py:25
  49.9 0.5 against.1.right_ref
  50.3 1.5 %collective-permute-done.3.other_ref = bf16[8,136,384]{2,1,0:T(8,128)(2,1)S(1)} collective-permute-done((bf16[8,136,384]{2,1,0:T(8,128)(2,1)S(1)}, bf16[8,136,384]{2,1,0:T(8,128)(2,1)S(1)}, u32[]{:S(2)}, u32[]{:S(2)}) %collective-permute-start.3) | collective-permute-done | bytes 835616 | tf_op jit(solution)/shard_map/ppermute | solution.py:25
  51.8 0.7 project.1
  52.6 10.7 %all_to_all.21.in_ref = bf16[8,64,384]{2,1,0:T(8,128)(2,1)S(1)} all-to-all(bf16[8,64,384]{2,1,0:T(8,128)(2,1)S(1)} %get-tuple-element.25), channel_id=1, replica_groups={{0,2,4,6,8,10,12,14},{1,3,5,7,9,11,13,15},{16,18,20,22,24,26,28,30},{17..., dimensions={0} | all-to-all | bytes 786432 | tf_op jit(solution)/shard_map/all_to_all | solution.py:33
  63.3 10.3 %all_to_all.22.whole_ref = bf16[8,64,384]{2,1,0:T(8,128)(2,1)S(1)} all-to-all(bf16[8,64,384]{2,1,0:T(8,128)(2,1)S(1)} %add_and_copy.1), channel_id=1, replica_groups={{0,2,4,6,8,10,12,14},{1,3,5,7,9,11,13,15},{16,18,20,22,24,26,28,30},{17..., dimensions={0} | all-to-all | bytes 786432 | tf_op jit(solution)/shard_map/all_to_all | solution.py:33
  73.6 0.5 meet.1
  74.1 3.8 %all-gather.1 = f32[128,256]{1,0:T(8,128)S(1)} all-gather(f32[64,256]{1,0:T(8,128)S(1)} %meet.1), channel_id=3, replica_groups={{0,1},{2,3},{4,5},{6,7},{8,9},{10,11},{12,13},{14,15},{16,17},{18,19},{..., dimensions={0}, use_global_device_ids=true | all-gather | bytes 196608 | tf_op jit(solution)/shard_map/all_gather | solution.py:29
  77.9 1.9 %collective-permute-start.4 = (bf16[64,128]{1,0:T(8,128)(2,1)S(1)}, bf16[64,128]{1,0:T(8,128)(2,1)S(1)}, u32[]{:S(2)}, u32[]{:S(2)}) collective-permute-start(bf16[64,128]{1,0:T(8,128)(2,1)S(1)} %add_met.1), channel_id=1, source_target_pairs={{0,16},{16,32},{32,48},{48,64},{64,80},{80,96},{96,112},{112,128},... | collective-permute-start | bytes 49160 | tf_op jit(solution)/shard_map/ppermute | solution.py:21
  79.8 2.3 %residual.1 = bf16[136,6144]{1,0:T(8,128)(2,1)} custom-call(s32[1]{0:T(128)} %bitcast.core_ref, bf16[136,6144]{1,0:T(8,128)(2,1)S(1)} %bitcast.16, bf16[2,64,256]{2,1,0:T(8,128)(2,1)S(1)} %factors_of.1.factors_ref), custom_call_target="tpu_custom_call" | custom-call | flops 213909504 | bytes 1048576 | tf_op jit(solution)/shard_map/residual/pallas_call | solution.py:219
  82.1 4.6 %collective-permute-done.4.met_ref = bf16[64,128]{1,0:T(8,128)(2,1)S(1)} collective-permute-done((bf16[64,128]{1,0:T(8,128)(2,1)S(1)}, bf16[64,128]{1,0:T(8,128)(2,1)S(1)}, u32[]{:S(2)}, u32[]{:S(2)}) %collective-permute-start.4) | collective-permute-done | bytes 16416 | tf_op jit(solution)/shard_map/ppermute | solution.py:21
  87.0 9.4 %all_to_all.23.in_ref = bf16[8,64,384]{2,1,0:T(8,128)(2,1)S(1)} all-to-all(bf16[8,64,384]{2,1,0:T(8,128)(2,1)S(1)} %expand.1), channel_id=1, replica_groups={{0,2,4,6,8,10,12,14},{1,3,5,7,9,11,13,15},{16,18,20,22,24,26,28,30},{17..., dimensions={0} | all-to-all | bytes 786432 | tf_op jit(solution)/shard_map/all_to_all | solution.py:33
  96.4 3.9 %collective-permute-start.5 = (bf16[64,384]{1,0:T(8,128)(2,1)S(1)}, bf16[64,384]{1,0:T(8,128)(2,1)S(1)}, u32[]{:S(2)}, u32[]{:S(2)}) collective-permute-start(bf16[64,384]{1,0:T(8,128)(2,1)S(1)} %add_up.1), channel_id=1, source_target_pairs={{0,496},{16,0},{32,16},{48,32},{64,48},{80,64},{96,80},{112,96},{1... | collective-permute-start | bytes 147464 | tf_op jit(solution)/shard_map/ppermute | solution.py:21
  100.3 2.3 %factor.1.inverse_ref = f32[64,64]{1,0:T(8,128)S(1)} custom-call(f32[2,64,256]{2,1,0:T(8,128)S(1)} %bitcast.19), custom_call_target="tpu_custom_call" | custom-call | flops 427819008 | bytes 1048576 | tf_op jit(solution)/shard_map/factor/pallas_call | solution.py:230
  102.7 0.9 finish.1
  (17 shorter events, 0.9 us)
Async XLA Ops:
  0.6 16.6 %collective-permute-start = (bf16[64,384]{1,0:T(8,128)(2,1)}, bf16[64,384]{1,0:T(8,128)(2,1)S(1)}, u32[]{:S(2)}, u32[]{:S(2)}) collective-permute-start(bf16[64,384]{1,0:T(8,128)(2,1)} %bitcast.24), channel_id=1, source_target_pairs={{0,16},{16,32},{32,48},{48,64},{64,80},{80,96},{96,112},{112,128},... | collective-permute-start | bytes 147464 | tf_op jit(solution)/shard_map/ppermute | solution.py:21
  7.3 1.4 %copy-start = (bf16[1,136,6144]{2,1,0:T(8,128)(2,1)S(1)}, bf16[1,136,6144]{2,1,0:T(8,128)(2,1)}, u32[]{:S(2)}) copy-start(bf16[1,136,6144]{2,1,0:T(8,128)(2,1)} %param.4) | copy-start | bytes 5013508
  8.7 8.5 %copy-start.3 = (bf16[1,384,64]{1,2,0:T(8,128)(2,1)S(1)}, bf16[1,384,64]{1,2,0:T(8,128)(2,1)}, u32[]{:S(2)}) copy-start(bf16[1,384,64]{1,2,0:T(8,128)(2,1)} %param.6) | copy-start | bytes 147460
  8.9 8.4 %collective-permute-start.1 = (bf16[8,136,384]{2,1,0:T(8,128)(2,1)S(1)}, bf16[8,136,384]{2,1,0:T(8,128)(2,1)S(1)}, u32[]{:S(2)}, u32[]{:S(2)}) collective-permute-start(bf16[8,136,384]{2,1,0:T(8,128)(2,1)S(1)} %get-tuple-element.17), channel_id=1, source_target_pairs={{0,1},{1,0},{2,3},{3,2},{4,5},{5,4},{6,7},{7,6},{8,9},{9,8},{10,11... | collective-permute-start | bytes 2506760 | tf_op jit(solution)/shard_map/ppermute | solution.py:25
  32.9 14.2 %copy-start.2 = (bf16[1,136,6144]{2,1,0:T(8,128)(2,1)S(1)}, bf16[1,136,6144]{2,1,0:T(8,128)(2,1)}, u32[]{:S(2)}) copy-start(bf16[1,136,6144]{2,1,0:T(8,128)(2,1)} %param.5) | copy-start | bytes 5013508
  41.2 9.1 %collective-permute-start.2 = (bf16[2,64,256]{2,1,0:T(8,128)(2,1)S(1)}, bf16[2,64,256]{2,1,0:T(8,128)(2,1)S(1)}, u32[]{:S(2)}, u32[]{:S(2)}) collective-permute-start(bf16[2,64,256]{2,1,0:T(8,128)(2,1)S(1)} %factors_of.1.factors_ref), channel_id=1, source_target_pairs={{0,496},{16,0},{32,16},{48,32},{64,48},{80,64},{96,80},{112,96},{1... | collective-permute-start | bytes 196616 | tf_op jit(solution)/shard_map/ppermute | solution.py:21
  47.3 4.5 %collective-permute-start.3 = (bf16[8,136,384]{2,1,0:T(8,128)(2,1)S(1)}, bf16[8,136,384]{2,1,0:T(8,128)(2,1)S(1)}, u32[]{:S(2)}, u32[]{:S(2)}) collective-permute-start(bf16[8,136,384]{2,1,0:T(8,128)(2,1)S(1)} %get-tuple-element.22), channel_id=1, source_target_pairs={{0,1},{1,0},{2,3},{3,2},{4,5},{5,4},{6,7},{7,6},{8,9},{9,8},{10,11... | collective-permute-start | bytes 2506760 | tf_op jit(solution)/shard_map/ppermute | solution.py:25
  63.2 16.6 %copy-start.1 = (bf16[1,136,6144]{2,1,0:T(8,128)(2,1)S(1)}, bf16[1,136,6144]{2,1,0:T(8,128)(2,1)}, u32[]{:S(2)}) copy-start(bf16[1,136,6144]{2,1,0:T(8,128)(2,1)} %param.4) | copy-start | bytes 5013508
  77.9 8.8 %collective-permute-start.4 = (bf16[64,128]{1,0:T(8,128)(2,1)S(1)}, bf16[64,128]{1,0:T(8,128)(2,1)S(1)}, u32[]{:S(2)}, u32[]{:S(2)}) collective-permute-start(bf16[64,128]{1,0:T(8,128)(2,1)S(1)} %add_met.1), channel_id=1, source_target_pairs={{0,16},{16,32},{32,48},{48,64},{64,80},{80,96},{96,112},{112,128},... | collective-permute-start | bytes 49160 | tf_op jit(solution)/shard_map/ppermute | solution.py:21
  96.4 6.3 %collective-permute-start.5 = (bf16[64,384]{1,0:T(8,128)(2,1)S(1)}, bf16[64,384]{1,0:T(8,128)(2,1)S(1)}, u32[]{:S(2)}, u32[]{:S(2)}) collective-permute-start(bf16[64,384]{1,0:T(8,128)(2,1)S(1)} %add_up.1), channel_id=1, source_target_pairs={{0,496},{16,0},{32,16},{48,32},{64,48},{80,64},{96,80},{112,96},{1... | collective-permute-start | bytes 147464 | tf_op jit(solution)/shard_map/ppermute | solution.py:21

commit v5 on v4

--- a/solution.py
+++ b/solution.py
@@ -1,3 +1,5 @@
+import functools
+
 import jax
 import jax.numpy as jnp
 from jax import lax
@@ -125,15 +127,19 @@
         term_ref[i] = lax.dot_general(inner, out_ref[i], TN, preferred_element_type=F32).astype(BF16)
 
 
-def residual(core_ref, micro_ref, factors_ref, error_ref, right_ref):
+def residual(first, core_ref, micro_ref, factors_ref, *refs):
+    error_ref, part_ref, sem = refs[-3:]
     left = factors_ref[core_ref[0], :, :ROWS]
     upright = left.astype(F32).T.astype(BF16)
-    strips = [slice(j * SLICE, (j + 1) * SLICE) for j in range(DP)]
-    for at in strips:
-        right_ref[:, at] = jnp.dot(left, micro_ref[:, at], preferred_element_type=F32).astype(BF16)
-    for at in strips:
-        approx = jnp.dot(upright, right_ref[:, at], preferred_element_type=F32)
-        error_ref[:, at] = (micro_ref[:, at].astype(F32) - approx).astype(BF16)
+    strips = [slice(j * SLICE, (j + 1) * SLICE) for j in range(HALF)]
+    micro = [micro_ref[:, first + j * SLICE : first + (j + 1) * SLICE] for j in range(HALF)]
+    right = [jnp.dot(left, part, preferred_element_type=F32).astype(BF16) for part in micro]
+    for at, rows, part in zip(strips, micro, right):
+        approx = jnp.dot(upright, part, preferred_element_type=F32)
+        part_ref[:, at] = (rows.astype(F32) - approx).astype(BF16)
+    move = pltpu.make_async_copy(part_ref, error_ref.at[:, first : first + D // 2], sem)
+    move.start()
+    move.wait()
 
 
 def add_up(in_ref, out_ref):
@@ -179,6 +185,7 @@
 
 LONG = 2**36
 VMEM = pl.BlockSpec(memory_space=pltpu.VMEM)
+ANY = pl.BlockSpec(memory_space=pl.ANY)
 SMEM = pl.BlockSpec(memory_space=pltpu.SMEM)
 
 
@@ -196,6 +203,20 @@
     )
 
 
+def remainder(first, core, micro, factors, *before):
+    return pl.pallas_call(
+        functools.partial(residual, first),
+        out_shape=jax.ShapeDtypeStruct((ROWS, D), BF16),
+        in_specs=[SMEM, VMEM, VMEM] + [ANY] * len(before),
+        out_specs=ANY,
+        scratch_shapes=[pltpu.VMEM((ROWS, D // 2), BF16), pltpu.SemaphoreType.DMA],
+        input_output_aliases={3: 0} if before else {},
+        compiler_params=pltpu.CompilerParams(vmem_limit_bytes=10 * 2**20),
+        cost_estimate=pl.CostEstimate(flops=2 * ROWS * D * RANK, bytes_accessed=2**20, transcendentals=0),
+        name="residual",
+    )(core, micro, factors, *before)
+
+
 def local(corrected, inputs, act_basis, weight_basis):
     micro, rows = corrected[0], inputs[0]
     core = (lax.axis_index("dp") % 2).reshape(1)
@@ -207,23 +228,23 @@
     warm = passed_along(weight_basis[0].T, 1)
     micro_own, micro_other = kernel(split_halves, halves, halves)(core, micro)
     micro_other = exchanged(micro_other)
+    rows_own, rows_other = kernel(split_halves, halves, halves)(core, rows)
+    rows_other = exchanged(rows_other)
     both = kernel(copies, stacked, flops=LONG)(act_basis[0].T, warm)
     both, micro_other = lax.optimization_barrier((both, micro_other))
-    both = across(both)
+    both, rows_other = lax.optimization_barrier((across(both), rows_other))
     part = kernel(half_product, ((2, ROWS, 2 * RANK), F32), flops=2 * product)(core, micro_own, micro_other, both)
     factors = kernel(factors_of, ((2, RANK, 256), BF16), flops=4 * product)(both_cores(part))
     factors_in = passed_along(factors, -1)
-    rows_own, rows_other = kernel(split_halves, halves, halves)(core, lax.optimization_barrier((rows, factors))[0])
-    rows_other = exchanged(rows_other)
-    right = kernel(against, stacked, flops=LONG)(core, micro_own, micro_other, factors)
-    error = kernel(residual, ((ROWS, D), BF16), flops=2 * product, scratch=[pltpu.VMEM((RANK, D), BF16)])(
-        core, micro, factors
-    )
-    factors_in, rows_other, right = lax.optimization_barrier((factors_in, rows_other, right))
+    right = kernel(against, stacked, flops=product)(core, micro_own, micro_other, factors)
+    error = remainder(0, core, micro, factors)
+    factors_in, rows_other, right, error = lax.optimization_barrier((factors_in, rows_other, right, error))
     terms, summed = kernel(project, stacked, blocks, flops=product)(core, rows_own, rows_other, factors_in)
     whole = across(kernel(add_and_copy, blocks)(across(summed)))
     met = both_cores(kernel(meet, ((RANK, 256), F32), flops=product)(whole, terms))
     met_in = passed_along(kernel(add_met, ((RANK, 2 * RANK), BF16))(met), 1)
+    met, error = lax.optimization_barrier((met, error))
+    error = remainder(D // 2, core, micro, factors, error)
     met_in, error = lax.optimization_barrier((met_in, error))
     parts = across(kernel(expand, blocks, flops=product)(met_in, right))
     parts = passed_along(kernel(add_up, ((RANK, SLICE), BF16))(parts), -1)

time: 105 us -> 103 us (0.981)
  blocking collectives: 54.2 us -> 38.4 us
  starting transfers between devices: 24.9 us -> 31.3 us
  waiting for transfers between devices: 10.4 us -> 14.2 us
  local copies, waits for them, and re-layouts: 1.45 us -> 3.79 us
  Pallas kernels: 11.7 us -> 13.4 us
    all_to_all x4 -> x3, blocking collectives: 45.9 us -> 29.6 us  [across(): lax.all_to_all(blocks, 'dp', 0, 0, tiled=True, axis_index_groups=ACROSS)]
    all_to_all x0 -> x1, starting transfers between devices: none -> 4.82 us  [across(): lax.all_to_all(blocks, 'dp', 0, 0, tiled=True, axis_index_groups=ACROSS)]
    all_to_all x0 -> x1, waiting for transfers between devices: none -> 2.71 us  [across(): lax.all_to_all(blocks, 'dp', 0, 0, tiled=True, axis_index_groups=ACROSS)]
    unnamed x8 -> x12, local copies, waits for them, and re-layouts: 1.45 us -> 3.79 us
    ppermute x2, starting transfers between devices: 6.6 us -> 7.92 us  [exchanged(): return lax.ppermute(shard, 'dp', [(i, i ^ 1) for i in range(DP)])]
    pallas_call x3 -> x4, Pallas kernels: 2.88 us -> 3.68 us  [the longest x2 3.06 us: remainder(): pl.pallas_call(functools.partial(residual, first), out_shape=jax.ShapeDty...]
  transfers between devices with their start and end apart: 6 -> 7, of which waited for: 4 -> 6; matrix products, arithmetic and copies ran while one was open for 0% -> 0% of each run, Pallas kernels for 5% -> 7%
where the time goes in v5:
time: 103 us; the launch traced here: 102 us
  blocking collectives  38.4 us (37%)
  starting transfers between devices  31.3 us (30%)
  waiting for transfers between devices  14.2 us (14%)
  Pallas kernels  13.4 us (13%)
  local copies, waits for them, and re-layouts  3.79 us (4%)
    all_to_all x3, blocking collectives, across(): lax.all_to_all(blocks, 'dp', 0, 0, tiled=True, axis_index_groups=ACROSS)  29.6 us
    ppermute x4, starting transfers between devices, passed_along(): lax.ppermute(shard, 'pipe', [(i, (i + by) % devices) for i in range(devic...  18.6 us
    ppermute x4, waiting for transfers between devices, passed_along(): lax.ppermute(shard, 'pipe', [(i, (i + by) % devices) for i in range(devic...  9.51 us
    all_gather x2, blocking collectives, both_cores(): return lax.all_gather(shard, 'dp', axis_index_groups=CORES)  8.85 us
    ppermute x2, starting transfers between devices, exchanged(): return lax.ppermute(shard, 'dp', [(i, i ^ 1) for i in range(DP)])  7.92 us
    all_to_all x1, starting transfers between devices, across(): lax.all_to_all(blocks, 'dp', 0, 0, tiled=True, axis_index_groups=ACROSS)  4.82 us
    unnamed x12, local copies, waits for them, and re-layouts  3.79 us
    pallas_call x1, Pallas kernels, local(): kernel(factors_of, ((2, RANK, 256), BF16), flops=4 * product)  3.16 us
  transfers between devices with their start and end apart: 7, of which 6 were waited for; matrix products, arithmetic and copies ran while one was open for 0% of the time, Pallas kernels for 7%

profile of v5, /device:TPU:1, one launch (start us, length us, event | category | flops | bytes accessed | tf_op | source)
XLA Modules:
  0.0 101.8 jit_solution(12582916420703983772)
XLA Ops:
  0.6 6.6 %collective-permute-start = (bf16[64,384]{1,0:T(8,128)(2,1)}, bf16[64,384]{1,0:T(8,128)(2,1)S(1)}, u32[]{:S(2)}, u32[]{:S(2)}) collective-permute-start(bf16[64,384]{1,0:T(8,128)(2,1)} %bitcast.25), channel_id=1, source_target_pairs={{0,16},{16,32},{32,48},{48,64},{64,80},{80,96},{96,112},{112,128},... | collective-permute-start | bytes 147464 | tf_op jit(solution)/shard_map/ppermute | solution.py:23
  7.3 1.4 %copy-done = bf16[1,136,6144]{2,1,0:T(8,128)(2,1)S(1)} copy-done((bf16[1,136,6144]{2,1,0:T(8,128)(2,1)S(1)}, bf16[1,136,6144]{2,1,0:T(8,128)(2,1)}, u32[]{:S(2)}) %copy-start) | copy-done | bytes 1671192
  8.9 4.1 %collective-permute-start.1 = (bf16[8,136,384]{2,1,0:T(8,128)(2,1)S(1)}, bf16[8,136,384]{2,1,0:T(8,128)(2,1)S(1)}, u32[]{:S(2)}, u32[]{:S(2)}) collective-permute-start(bf16[8,136,384]{2,1,0:T(8,128)(2,1)S(1)} %get-tuple-element.22), channel_id=1, source_target_pairs={{0,1},{1,0},{2,3},{3,2},{4,5},{5,4},{6,7},{7,6},{8,9},{9,8},{10,11... | collective-permute-start | bytes 2506760 | tf_op jit(solution)/shard_map/ppermute | solution.py:27
  13.0 4.3 %collective-permute-done.two_ref = bf16[64,384]{1,0:T(8,128)(2,1)S(1)} collective-permute-done((bf16[64,384]{1,0:T(8,128)(2,1)}, bf16[64,384]{1,0:T(8,128)(2,1)S(1)}, u32[]{:S(2)}, u32[]{:S(2)}) %collective-permute-start) | collective-permute-done | bytes 49184 | tf_op jit(solution)/shard_map/ppermute | solution.py:23
  17.2 0.9 copies.1
  18.2 4.8 %all-to-all-start = ((bf16[8,128,384]{2,1,0:T(8,128)(2,1)}), bf16[8,128,384]{2,1,0:T(8,128)(2,1)S(1)}, u32[]{:S(2)}, u32[]{:S(2)}) async-start(bf16[8,128,384]{2,1,0:T(8,128)(2,1)} %copies.1), calls=%async_computation | async-start | bytes 1572864 | tf_op jit(solution)/shard_map/all_to_all | solution.py:35
  23.0 1.4 %copy-done.2 = bf16[1,136,6144]{2,1,0:T(8,128)(2,1)S(1)} copy-done((bf16[1,136,6144]{2,1,0:T(8,128)(2,1)S(1)}, bf16[1,136,6144]{2,1,0:T(8,128)(2,1)}, u32[]{:S(2)}) %copy-start.2) | copy-done | bytes 1671192
  24.6 3.9 %collective-permute-start.2 = (bf16[8,136,384]{2,1,0:T(8,128)(2,1)S(1)}, bf16[8,136,384]{2,1,0:T(8,128)(2,1)S(1)}, u32[]{:S(2)}, u32[]{:S(2)}) collective-permute-start(bf16[8,136,384]{2,1,0:T(8,128)(2,1)S(1)} %get-tuple-element.25), channel_id=1, source_target_pairs={{0,1},{1,0},{2,3},{3,2},{4,5},{5,4},{6,7},{7,6},{8,9},{9,8},{10,11... | collective-permute-start | bytes 2506760 | tf_op jit(solution)/shard_map/ppermute | solution.py:27
  28.5 2.0 %collective-permute-done.2.other_ref = bf16[8,136,384]{2,1,0:T(8,128)(2,1)S(1)} collective-permute-done((bf16[8,136,384]{2,1,0:T(8,128)(2,1)S(1)}, bf16[8,136,384]{2,1,0:T(8,128)(2,1)S(1)}, u32[]{:S(2)}, u32[]{:S(2)}) %collective-permute-start.2) | collective-permute-done | bytes 835616 | tf_op jit(solution)/shard_map/ppermute | solution.py:27
  31.3 2.7 %all-to-all-done.both_ref = bf16[8,128,384]{2,1,0:T(8,128)(2,1)S(1)} async-done(((bf16[8,128,384]{2,1,0:T(8,128)(2,1)}), bf16[8,128,384]{2,1,0:T(8,128)(2,1)S(1)}, u32[]{:S(2)}, u32[]{:S(2)}) %all-to-all-start) | async-done | bytes 786464 | tf_op jit(solution)/shard_map/all_to_all | solution.py:35
  34.7 4.5 %all-gather = f32[4,136,128]{2,1,0:T(8,128)S(1)} all-gather(f32[2,136,128]{2,1,0:T(8,128)S(1)} %half_product.1), channel_id=2, replica_groups={{0,1},{2,3},{4,5},{6,7},{8,9},{10,11},{12,13},{14,15},{16,17},{18,19},{..., dimensions={0}, use_global_device_ids=true | all-gather | bytes 417792 | tf_op jit(solution)/shard_map/all_gather | solution.py:31
  39.2 3.2 %factors_of.1.factors_ref = bf16[2,64,256]{2,1,0:T(8,128)(2,1)S(1)} custom-call(f32[2,2,136,128]{3,2,1,0:T(8,128)S(1)} %bitcast.21), custom_call_target="tpu_custom_call" | custom-call | flops 427819008 | bytes 1048576 | tf_op jit(solution)/shard_map/factors_of/pallas_call | solution.py:237
  42.4 4.9 %collective-permute-start.3 = (bf16[2,64,256]{2,1,0:T(8,128)(2,1)S(1)}, bf16[2,64,256]{2,1,0:T(8,128)(2,1)S(1)}, u32[]{:S(2)}, u32[]{:S(2)}) collective-permute-start(bf16[2,64,256]{2,1,0:T(8,128)(2,1)S(1)} %factors_of.1.factors_ref), channel_id=1, source_target_pairs={{0,496},{16,0},{32,16},{48,32},{64,48},{80,64},{96,80},{112,96},{1... | collective-permute-start | bytes 196616 | tf_op jit(solution)/shard_map/ppermute | solution.py:23
  47.8 1.5 %residual.2.refs_0_ = bf16[136,6144]{1,0:T(8,128)(2,1)} custom-call(s32[1]{0:T(128)} %bitcast.core_ref, bf16[136,6144]{1,0:T(8,128)(2,1)S(1)} %bitcast.16, bf16[2,64,256]{2,1,0:T(8,128)(2,1)S(1)} %factors_of.1.factors_ref), custom_call_target="tpu_custom_call" | custom-call | flops 106954752 | bytes 1048576 | tf_op jit(solution)/shard_map/residual/pallas_call | solution.py:207
  49.4 1.0 %collective-permute-done.3.factors_ref = bf16[2,64,256]{2,1,0:T(8,128)(2,1)S(1)} collective-permute-done((bf16[2,64,256]{2,1,0:T(8,128)(2,1)S(1)}, bf16[2,64,256]{2,1,0:T(8,128)(2,1)S(1)}, u32[]{:S(2)}, u32[]{:S(2)}) %collective-permute-start.3) | collective-permute-done | bytes 65568 | tf_op jit(solution)/shard_map/ppermute | solution.py:23
  51.1 10.4 %all_to_all.20.in_ref = bf16[8,64,384]{2,1,0:T(8,128)(2,1)S(1)} all-to-all(bf16[8,64,384]{2,1,0:T(8,128)(2,1)S(1)} %get-tuple-element.30), channel_id=1, replica_groups={{0,2,4,6,8,10,12,14},{1,3,5,7,9,11,13,15},{16,18,20,22,24,26,28,30},{17..., dimensions={0} | all-to-all | bytes 786432 | tf_op jit(solution)/shard_map/all_to_all | solution.py:35
  61.6 9.5 %all_to_all.21.whole_ref = bf16[8,64,384]{2,1,0:T(8,128)(2,1)S(1)} all-to-all(bf16[8,64,384]{2,1,0:T(8,128)(2,1)S(1)} %add_and_copy.1), channel_id=1, replica_groups={{0,2,4,6,8,10,12,14},{1,3,5,7,9,11,13,15},{16,18,20,22,24,26,28,30},{17..., dimensions={0} | all-to-all | bytes 786432 | tf_op jit(solution)/shard_map/all_to_all | solution.py:35
  71.6 4.3 %all-gather.1 = f32[128,256]{1,0:T(8,128)S(1)} all-gather(f32[64,256]{1,0:T(8,128)S(1)} %meet.1), channel_id=3, replica_groups={{0,1},{2,3},{4,5},{6,7},{8,9},{10,11},{12,13},{14,15},{16,17},{18,19},{..., dimensions={0}, use_global_device_ids=true | all-gather | bytes 196608 | tf_op jit(solution)/shard_map/all_gather | solution.py:31
  75.9 3.8 %collective-permute-start.4 = (bf16[64,128]{1,0:T(8,128)(2,1)S(1)}, bf16[64,128]{1,0:T(8,128)(2,1)S(1)}, u32[]{:S(2)}, u32[]{:S(2)}) collective-permute-start(bf16[64,128]{1,0:T(8,128)(2,1)S(1)} %add_met.1), channel_id=1, source_target_pairs={{0,16},{16,32},{32,48},{48,64},{64,80},{80,96},{96,112},{112,128},... | collective-permute-start | bytes 49160 | tf_op jit(solution)/shard_map/ppermute | solution.py:23
  79.7 1.5 %residual.3 = bf16[136,6144]{1,0:T(8,128)(2,1)} custom-call(s32[1]{0:T(128)} %bitcast.core_ref, bf16[136,6144]{1,0:T(8,128)(2,1)S(1)} %bitcast.17, bf16[2,64,256]{2,1,0:T(8,128)(2,1)S(1)} %factors_of.1.factors_ref, bf16[136,6144]{1,0:T(8,128)(2,1)} %residual.2.refs_0_), custom_call_target="tpu_custom_call", output_to_operand_aliasing={{}: (3, {})} | custom-call | flops 106954752 | bytes 1048576 | tf_op jit(solution)/shard_map/residual/pallas_call | solution.py:207
  81.3 3.4 %collective-permute-done.4.met_ref = bf16[64,128]{1,0:T(8,128)(2,1)S(1)} collective-permute-done((bf16[64,128]{1,0:T(8,128)(2,1)S(1)}, bf16[64,128]{1,0:T(8,128)(2,1)S(1)}, u32[]{:S(2)}, u32[]{:S(2)}) %collective-permute-start.4) | collective-permute-done | bytes 16416 | tf_op jit(solution)/shard_map/ppermute | solution.py:23
  85.0 9.7 %all_to_all.22.in_ref = bf16[8,64,384]{2,1,0:T(8,128)(2,1)S(1)} all-to-all(bf16[8,64,384]{2,1,0:T(8,128)(2,1)S(1)} %expand.1), channel_id=1, replica_groups={{0,2,4,6,8,10,12,14},{1,3,5,7,9,11,13,15},{16,18,20,22,24,26,28,30},{17..., dimensions={0} | all-to-all | bytes 786432 | tf_op jit(solution)/shard_map/all_to_all | solution.py:35
  94.7 3.2 %collective-permute-start.5 = (bf16[64,384]{1,0:T(8,128)(2,1)S(1)}, bf16[64,384]{1,0:T(8,128)(2,1)S(1)}, u32[]{:S(2)}, u32[]{:S(2)}) collective-permute-start(bf16[64,384]{1,0:T(8,128)(2,1)S(1)} %add_up.1), channel_id=1, source_target_pairs={{0,496},{16,0},{32,16},{48,32},{64,48},{80,64},{96,80},{112,96},{1... | collective-permute-start | bytes 147464 | tf_op jit(solution)/shard_map/ppermute | solution.py:23
  97.9 2.3 %factor.1.inverse_ref = f32[64,64]{1,0:T(8,128)S(1)} custom-call(f32[2,64,256]{2,1,0:T(8,128)S(1)} %bitcast.20), custom_call_target="tpu_custom_call" | custom-call | flops 427819008 | bytes 1048576 | tf_op jit(solution)/shard_map/factor/pallas_call | solution.py:251
  (23 shorter events, 5.6 us)
Async XLA Ops:
  0.6 16.6 %collective-permute-start = (bf16[64,384]{1,0:T(8,128)(2,1)}, bf16[64,384]{1,0:T(8,128)(2,1)S(1)}, u32[]{:S(2)}, u32[]{:S(2)}) collective-permute-start(bf16[64,384]{1,0:T(8,128)(2,1)} %bitcast.25), channel_id=1, source_target_pairs={{0,16},{16,32},{32,48},{48,64},{64,80},{80,96},{96,112},{112,128},... | collective-permute-start | bytes 147464 | tf_op jit(solution)/shard_map/ppermute | solution.py:23
  7.3 1.4 %copy-start = (bf16[1,136,6144]{2,1,0:T(8,128)(2,1)S(1)}, bf16[1,136,6144]{2,1,0:T(8,128)(2,1)}, u32[]{:S(2)}) copy-start(bf16[1,136,6144]{2,1,0:T(8,128)(2,1)} %param.4) | copy-start | bytes 5013508
  8.7 8.5 %copy-start.5 = (bf16[1,384,64]{1,2,0:T(8,128)(2,1)S(1)}, bf16[1,384,64]{1,2,0:T(8,128)(2,1)}, u32[]{:S(2)}) copy-start(bf16[1,384,64]{1,2,0:T(8,128)(2,1)} %param.6) | copy-start | bytes 147460
  8.9 9.3 %collective-permute-start.1 = (bf16[8,136,384]{2,1,0:T(8,128)(2,1)S(1)}, bf16[8,136,384]{2,1,0:T(8,128)(2,1)S(1)}, u32[]{:S(2)}, u32[]{:S(2)}) collective-permute-start(bf16[8,136,384]{2,1,0:T(8,128)(2,1)S(1)} %get-tuple-element.22), channel_id=1, source_target_pairs={{0,1},{1,0},{2,3},{3,2},{4,5},{5,4},{6,7},{7,6},{8,9},{9,8},{10,11... | collective-permute-start | bytes 2506760 | tf_op jit(solution)/shard_map/ppermute | solution.py:27
  18.2 15.9 %all-to-all-start = ((bf16[8,128,384]{2,1,0:T(8,128)(2,1)}), bf16[8,128,384]{2,1,0:T(8,128)(2,1)S(1)}, u32[]{:S(2)}, u32[]{:S(2)}) async-start(bf16[8,128,384]{2,1,0:T(8,128)(2,1)} %copies.1), calls=%async_computation | async-start | bytes 1572864 | tf_op jit(solution)/shard_map/all_to_all | solution.py:35
  23.0 1.4 %copy-start.2 = (bf16[1,136,6144]{2,1,0:T(8,128)(2,1)S(1)}, bf16[1,136,6144]{2,1,0:T(8,128)(2,1)}, u32[]{:S(2)}) copy-start(bf16[1,136,6144]{2,1,0:T(8,128)(2,1)} %param.5) | copy-start | bytes 5013508
  24.6 5.8 %collective-permute-start.2 = (bf16[8,136,384]{2,1,0:T(8,128)(2,1)S(1)}, bf16[8,136,384]{2,1,0:T(8,128)(2,1)S(1)}, u32[]{:S(2)}, u32[]{:S(2)}) collective-permute-start(bf16[8,136,384]{2,1,0:T(8,128)(2,1)S(1)} %get-tuple-element.25), channel_id=1, source_target_pairs={{0,1},{1,0},{2,3},{3,2},{4,5},{5,4},{6,7},{7,6},{8,9},{9,8},{10,11... | collective-permute-start | bytes 2506760 | tf_op jit(solution)/shard_map/ppermute | solution.py:27
  30.4 0.9 copy-start.3
  39.2 8.6 %copy-start.1 = (bf16[1,136,6144]{2,1,0:T(8,128)(2,1)S(1)}, bf16[1,136,6144]{2,1,0:T(8,128)(2,1)}, u32[]{:S(2)}) copy-start(bf16[1,136,6144]{2,1,0:T(8,128)(2,1)} %param.4) | copy-start | bytes 5013508
  42.4 8.0 %collective-permute-start.3 = (bf16[2,64,256]{2,1,0:T(8,128)(2,1)S(1)}, bf16[2,64,256]{2,1,0:T(8,128)(2,1)S(1)}, u32[]{:S(2)}, u32[]{:S(2)}) collective-permute-start(bf16[2,64,256]{2,1,0:T(8,128)(2,1)S(1)} %factors_of.1.factors_ref), channel_id=1, source_target_pairs={{0,496},{16,0},{32,16},{48,32},{64,48},{80,64},{96,80},{112,96},{1... | collective-permute-start | bytes 196616 | tf_op jit(solution)/shard_map/ppermute | solution.py:23
  47.8 2.6 %copy-start.4 = (bf16[8,136,384]{2,1,0:T(8,128)(2,1)S(1)}, bf16[8,136,384]{2,1,0:T(8,128)(2,1)}, u32[]{:S(2)}) copy-start(bf16[8,136,384]{2,1,0:T(8,128)(2,1)} %copy-done.3) | copy-start | bytes 2506756
  75.9 8.8 %collective-permute-start.4 = (bf16[64,128]{1,0:T(8,128)(2,1)S(1)}, bf16[64,128]{1,0:T(8,128)(2,1)S(1)}, u32[]{:S(2)}, u32[]{:S(2)}) collective-permute-start(bf16[64,128]{1,0:T(8,128)(2,1)S(1)} %add_met.1), channel_id=1, source_target_pairs={{0,16},{16,32},{32,48},{48,64},{64,80},{80,96},{96,112},{112,128},... | collective-permute-start | bytes 49160 | tf_op jit(solution)/shard_map/ppermute | solution.py:23
  94.7 6.3 %collective-permute-start.5 = (bf16[64,384]{1,0:T(8,128)(2,1)S(1)}, bf16[64,384]{1,0:T(8,128)(2,1)S(1)}, u32[]{:S(2)}, u32[]{:S(2)}) collective-permute-start(bf16[64,384]{1,0:T(8,128)(2,1)S(1)} %add_up.1), channel_id=1, source_target_pairs={{0,496},{16,0},{32,16},{48,32},{64,48},{80,64},{96,80},{112,96},{1... | collective-permute-start | bytes 147464 | tf_op jit(solution)/shard_map/ppermute | solution.py:23

commit v6 on v5

--- a/solution.py
+++ b/solution.py
@@ -104,14 +104,26 @@
     gram = [lax.dot_general(a, a, NT, precision=HIGH, preferred_element_type=F32) for a in raw]
     inverse = [inverse_cholesky(a) for a in gram]
     warm = [lax.dot_general(both[:RANK], both[RANK:], NT, precision=HIGH, preferred_element_type=F32) for both in total]
+    wide = []
     for slot in range(2):
         both = jnp.concatenate([raw[slot], jnp.zeros((RANK, 192 - ROWS), F32), warm[slot]], axis=1)
-        out_ref[slot] = jnp.dot(inverse[slot], both, precision=HIGH, preferred_element_type=F32).astype(BF16)
+        wide.append(jnp.dot(inverse[slot], both, precision=HIGH, preferred_element_type=F32))
+    wide = jnp.concatenate(wide, axis=0)
+    rest = wide[:, 128:].T
+    out_ref[:128] = wide[:, :128].astype(BF16)
+    out_ref[128:192] = rest[RANK:].astype(BF16)
+    out_ref[192:] = rest[:16].astype(BF16)
+
+
+def left_of(factors_ref, core):
+    last = factors_ref[192:].astype(F32).T[:, : ROWS - 128].astype(BF16)
+    left = jnp.concatenate([factors_ref[:128], last], axis=1)
+    return jnp.where(core == 0, left[:RANK], left[RANK:])
 
 
 def against(core_ref, own_ref, other_ref, factors_ref, out_ref):
     core = core_ref[0]
-    own, other = factors_ref[core, :, :ROWS], factors_ref[1 - core, :, :ROWS]
+    own, other = left_of(factors_ref, core), left_of(factors_ref, 1 - core)
     at, to = pl.multiple_of(core * RANK, RANK), pl.multiple_of((1 - core) * RANK, RANK)
     for i in range(HALF):
         out_ref[i, pl.ds(at, RANK), :] = jnp.dot(
@@ -122,14 +134,13 @@
 
 def project(core_ref, own_ref, other_ref, factors_ref, out_ref, term_ref):
     against(core_ref, own_ref, other_ref, factors_ref, out_ref)
-    inner = jnp.concatenate([factors_ref[0, :, 192:], factors_ref[1, :, 192:]], axis=0)
-    for i in range(HALF):
-        term_ref[i] = lax.dot_general(inner, out_ref[i], TN, preferred_element_type=F32).astype(BF16)
+    for i in range(HALF):
+        term_ref[i] = jnp.dot(factors_ref[128:192], out_ref[i], preferred_element_type=F32).astype(BF16)
 
 
 def residual(first, core_ref, micro_ref, factors_ref, *refs):
     error_ref, part_ref, sem = refs[-3:]
-    left = factors_ref[core_ref[0], :, :ROWS]
+    left = left_of(factors_ref, core_ref[0])
     upright = left.astype(F32).T.astype(BF16)
     strips = [slice(j * SLICE, (j + 1) * SLICE) for j in range(HALF)]
     micro = [micro_ref[:, first + j * SLICE : first + (j + 1) * SLICE] for j in range(HALF)]
@@ -234,7 +245,7 @@
     both, micro_other = lax.optimization_barrier((both, micro_other))
     both, rows_other = lax.optimization_barrier((across(both), rows_other))
     part = kernel(half_product, ((2, ROWS, 2 * RANK), F32), flops=2 * product)(core, micro_own, micro_other, both)
-    factors = kernel(factors_of, ((2, RANK, 256), BF16), flops=4 * product)(both_cores(part))
+    factors = kernel(factors_of, ((208, 128), BF16), flops=4 * product)(both_cores(part))
     factors_in = passed_along(factors, -1)
     right = kernel(against, stacked, flops=product)(core, micro_own, micro_other, factors)
     error = remainder(0, core, micro, factors)

time: 103 us -> 103 us (level)
  no operation moved by 1% of the time
where the time goes in v6:
time: 103 us; the launch traced here: 101 us
  blocking collectives  38.4 us (37%)
  starting transfers between devices  31.2 us (30%)
  Pallas kernels  13.6 us (13%)
  waiting for transfers between devices  13.5 us (13%)
  local copies, waits for them, and re-layouts  3.79 us (4%)
    all_to_all x3, blocking collectives, across(): lax.all_to_all(blocks, 'dp', 0, 0, tiled=True, axis_index_groups=ACROSS)  29.2 us
    ppermute x4, starting transfers between devices, passed_along(): lax.ppermute(shard, 'pipe', [(i, (i + by) % devices) for i in range(devic...  18.5 us
    all_gather x2, blocking collectives, both_cores(): return lax.all_gather(shard, 'dp', axis_index_groups=CORES)  9.17 us
    ppermute x4, waiting for transfers between devices, passed_along(): lax.ppermute(shard, 'pipe', [(i, (i + by) % devices) for i in range(devic...  8.83 us
    ppermute x2, starting transfers between devices, exchanged(): return lax.ppermute(shard, 'dp', [(i, i ^ 1) for i in range(DP)])  7.92 us
    all_to_all x1, starting transfers between devices, across(): lax.all_to_all(blocks, 'dp', 0, 0, tiled=True, axis_index_groups=ACROSS)  4.82 us
    unnamed x12, local copies, waits for them, and re-layouts  3.79 us
    pallas_call x2, Pallas kernels, remainder(): pl.pallas_call(functools.partial(residual, first), out_shape=jax.ShapeDty...  3.2 us
  transfers between devices with their start and end apart: 7, of which 6 were waited for; matrix products, arithmetic and copies ran while one was open for 0% of the time, Pallas kernels for 7%

profile of v6, /device:TPU:1, one launch (start us, length us, event | category | flops | bytes accessed | tf_op | source)
XLA Modules:
  0.0 101.3 jit_solution(7114072660883266081)
XLA Ops:
  0.6 6.6 %collective-permute-start = (bf16[64,384]{1,0:T(8,128)(2,1)}, bf16[64,384]{1,0:T(8,128)(2,1)S(1)}, u32[]{:S(2)}, u32[]{:S(2)}) collective-permute-start(bf16[64,384]{1,0:T(8,128)(2,1)} %bitcast.25), channel_id=1, source_target_pairs={{0,16},{16,32},{32,48},{48,64},{64,80},{80,96},{96,112},{112,128},... | collective-permute-start | bytes 147464 | tf_op jit(solution)/shard_map/ppermute | solution.py:23
  7.3 1.4 %copy-done = bf16[1,136,6144]{2,1,0:T(8,128)(2,1)S(1)} copy-done((bf16[1,136,6144]{2,1,0:T(8,128)(2,1)S(1)}, bf16[1,136,6144]{2,1,0:T(8,128)(2,1)}, u32[]{:S(2)}) %copy-start) | copy-done | bytes 1671192
  8.9 4.1 %collective-permute-start.1 = (bf16[8,136,384]{2,1,0:T(8,128)(2,1)S(1)}, bf16[8,136,384]{2,1,0:T(8,128)(2,1)S(1)}, u32[]{:S(2)}, u32[]{:S(2)}) collective-permute-start(bf16[8,136,384]{2,1,0:T(8,128)(2,1)S(1)} %get-tuple-element.22), channel_id=1, source_target_pairs={{0,1},{1,0},{2,3},{3,2},{4,5},{5,4},{6,7},{7,6},{8,9},{9,8},{10,11... | collective-permute-start | bytes 2506760 | tf_op jit(solution)/shard_map/ppermute | solution.py:27
  13.0 4.3 %collective-permute-done.two_ref = bf16[64,384]{1,0:T(8,128)(2,1)S(1)} collective-permute-done((bf16[64,384]{1,0:T(8,128)(2,1)}, bf16[64,384]{1,0:T(8,128)(2,1)S(1)}, u32[]{:S(2)}, u32[]{:S(2)}) %collective-permute-start) | collective-permute-done | bytes 49184 | tf_op jit(solution)/shard_map/ppermute | solution.py:23
  17.2 0.9 copies.1
  18.2 4.8 %all-to-all-start = ((bf16[8,128,384]{2,1,0:T(8,128)(2,1)}), bf16[8,128,384]{2,1,0:T(8,128)(2,1)S(1)}, u32[]{:S(2)}, u32[]{:S(2)}) async-start(bf16[8,128,384]{2,1,0:T(8,128)(2,1)} %copies.1), calls=%async_computation | async-start | bytes 1572864 | tf_op jit(solution)/shard_map/all_to_all | solution.py:35
  23.0 1.4 %copy-done.2 = bf16[1,136,6144]{2,1,0:T(8,128)(2,1)S(1)} copy-done((bf16[1,136,6144]{2,1,0:T(8,128)(2,1)S(1)}, bf16[1,136,6144]{2,1,0:T(8,128)(2,1)}, u32[]{:S(2)}) %copy-start.2) | copy-done | bytes 1671192
  24.6 3.9 %collective-permute-start.2 = (bf16[8,136,384]{2,1,0:T(8,128)(2,1)S(1)}, bf16[8,136,384]{2,1,0:T(8,128)(2,1)S(1)}, u32[]{:S(2)}, u32[]{:S(2)}) collective-permute-start(bf16[8,136,384]{2,1,0:T(8,128)(2,1)S(1)} %get-tuple-element.25), channel_id=1, source_target_pairs={{0,1},{1,0},{2,3},{3,2},{4,5},{5,4},{6,7},{7,6},{8,9},{9,8},{10,11... | collective-permute-start | bytes 2506760 | tf_op jit(solution)/shard_map/ppermute | solution.py:27
  28.5 2.0 %collective-permute-done.2.other_ref = bf16[8,136,384]{2,1,0:T(8,128)(2,1)S(1)} collective-permute-done((bf16[8,136,384]{2,1,0:T(8,128)(2,1)S(1)}, bf16[8,136,384]{2,1,0:T(8,128)(2,1)S(1)}, u32[]{:S(2)}, u32[]{:S(2)}) %collective-permute-start.2) | collective-permute-done | bytes 835616 | tf_op jit(solution)/shard_map/ppermute | solution.py:27
  30.4 0.9 copy-done.3
  31.3 2.7 %all-to-all-done.both_ref = bf16[8,128,384]{2,1,0:T(8,128)(2,1)S(1)} async-done(((bf16[8,128,384]{2,1,0:T(8,128)(2,1)}), bf16[8,128,384]{2,1,0:T(8,128)(2,1)S(1)}, u32[]{:S(2)}, u32[]{:S(2)}) %all-to-all-start) | async-done | bytes 786464 | tf_op jit(solution)/shard_map/all_to_all | solution.py:35
  34.7 4.5 %all-gather = f32[4,136,128]{2,1,0:T(8,128)S(1)} all-gather(f32[2,136,128]{2,1,0:T(8,128)S(1)} %half_product.1), channel_id=2, replica_groups={{0,1},{2,3},{4,5},{6,7},{8,9},{10,11},{12,13},{14,15},{16,17},{18,19},{..., dimensions={0}, use_global_device_ids=true | all-gather | bytes 417792 | tf_op jit(solution)/shard_map/all_gather | solution.py:31
  39.2 3.1 %factors_of.1.factors_ref = bf16[208,128]{1,0:T(8,128)(2,1)S(1)} custom-call(f32[2,2,136,128]{3,2,1,0:T(8,128)S(1)} %bitcast.21), custom_call_target="tpu_custom_call" | custom-call | flops 427819008 | bytes 1048576 | tf_op jit(solution)/shard_map/factors_of/pallas_call | solution.py:248
  42.3 5.0 %collective-permute-start.3 = (bf16[208,128]{1,0:T(8,128)(2,1)S(1)}, bf16[208,128]{1,0:T(8,128)(2,1)S(1)}, u32[]{:S(2)}, u32[]{:S(2)}) collective-permute-start(bf16[208,128]{1,0:T(8,128)(2,1)S(1)} %factors_of.1.factors_ref), channel_id=1, source_target_pairs={{0,496},{16,0},{32,16},{48,32},{64,48},{80,64},{96,80},{112,96},{1... | collective-permute-start | bytes 159752 | tf_op jit(solution)/shard_map/ppermute | solution.py:23
  47.9 1.6 %residual.2.refs_0_ = bf16[136,6144]{1,0:T(8,128)(2,1)} custom-call(s32[1]{0:T(128)} %bitcast.core_ref, bf16[136,6144]{1,0:T(8,128)(2,1)S(1)} %bitcast.16, bf16[208,128]{1,0:T(8,128)(2,1)S(1)} %factors_of.1.factors_ref), custom_call_target="tpu_custom_call" | custom-call | flops 106954752 | bytes 1048576 | tf_op jit(solution)/shard_map/residual/pallas_call | solution.py:218
  50.6 10.1 %all_to_all.20.in_ref = bf16[8,64,384]{2,1,0:T(8,128)(2,1)S(1)} all-to-all(bf16[8,64,384]{2,1,0:T(8,128)(2,1)S(1)} %get-tuple-element.30), channel_id=1, replica_groups={{0,2,4,6,8,10,12,14},{1,3,5,7,9,11,13,15},{16,18,20,22,24,26,28,30},{17..., dimensions={0} | all-to-all | bytes 786432 | tf_op jit(solution)/shard_map/all_to_all | solution.py:35
  60.8 9.4 %all_to_all.21.whole_ref = bf16[8,64,384]{2,1,0:T(8,128)(2,1)S(1)} all-to-all(bf16[8,64,384]{2,1,0:T(8,128)(2,1)S(1)} %add_and_copy.1), channel_id=1, replica_groups={{0,2,4,6,8,10,12,14},{1,3,5,7,9,11,13,15},{16,18,20,22,24,26,28,30},{17..., dimensions={0} | all-to-all | bytes 786432 | tf_op jit(solution)/shard_map/all_to_all | solution.py:35
  70.8 4.6 %all-gather.1 = f32[128,256]{1,0:T(8,128)S(1)} all-gather(f32[64,256]{1,0:T(8,128)S(1)} %meet.1), channel_id=3, replica_groups={{0,1},{2,3},{4,5},{6,7},{8,9},{10,11},{12,13},{14,15},{16,17},{18,19},{..., dimensions={0}, use_global_device_ids=true | all-gather | bytes 196608 | tf_op jit(solution)/shard_map/all_gather | solution.py:31
  75.4 3.5 %collective-permute-start.4 = (bf16[64,128]{1,0:T(8,128)(2,1)S(1)}, bf16[64,128]{1,0:T(8,128)(2,1)S(1)}, u32[]{:S(2)}, u32[]{:S(2)}) collective-permute-start(bf16[64,128]{1,0:T(8,128)(2,1)S(1)} %add_met.1), channel_id=1, source_target_pairs={{0,16},{16,32},{32,48},{48,64},{64,80},{80,96},{96,112},{112,128},... | collective-permute-start | bytes 49160 | tf_op jit(solution)/shard_map/ppermute | solution.py:23
  78.9 1.6 %residual.3 = bf16[136,6144]{1,0:T(8,128)(2,1)} custom-call(s32[1]{0:T(128)} %bitcast.core_ref, bf16[136,6144]{1,0:T(8,128)(2,1)S(1)} %bitcast.17, bf16[208,128]{1,0:T(8,128)(2,1)S(1)} %factors_of.1.factors_ref, bf16[136,6144]{1,0:T(8,128)(2,1)} %residual.2.refs_0_), custom_call_target="tpu_custom_call", output_to_operand_aliasing={{}: (3, {})} | custom-call | flops 106954752 | bytes 1048576 | tf_op jit(solution)/shard_map/residual/pallas_call | solution.py:218
  80.6 3.6 %collective-permute-done.4.met_ref = bf16[64,128]{1,0:T(8,128)(2,1)S(1)} collective-permute-done((bf16[64,128]{1,0:T(8,128)(2,1)S(1)}, bf16[64,128]{1,0:T(8,128)(2,1)S(1)}, u32[]{:S(2)}, u32[]{:S(2)}) %collective-permute-start.4) | collective-permute-done | bytes 16416 | tf_op jit(solution)/shard_map/ppermute | solution.py:23
  84.5 9.6 %all_to_all.22.in_ref = bf16[8,64,384]{2,1,0:T(8,128)(2,1)S(1)} all-to-all(bf16[8,64,384]{2,1,0:T(8,128)(2,1)S(1)} %expand.1), channel_id=1, replica_groups={{0,2,4,6,8,10,12,14},{1,3,5,7,9,11,13,15},{16,18,20,22,24,26,28,30},{17..., dimensions={0} | all-to-all | bytes 786432 | tf_op jit(solution)/shard_map/all_to_all | solution.py:35
  94.2 3.4 %collective-permute-start.5 = (bf16[64,384]{1,0:T(8,128)(2,1)S(1)}, bf16[64,384]{1,0:T(8,128)(2,1)S(1)}, u32[]{:S(2)}, u32[]{:S(2)}) collective-permute-start(bf16[64,384]{1,0:T(8,128)(2,1)S(1)} %add_up.1), channel_id=1, source_target_pairs={{0,496},{16,0},{32,16},{48,32},{64,48},{80,64},{96,80},{112,96},{1... | collective-permute-start | bytes 147464 | tf_op jit(solution)/shard_map/ppermute | solution.py:23
  97.5 2.3 %factor.1.inverse_ref = f32[64,64]{1,0:T(8,128)S(1)} custom-call(f32[2,64,256]{2,1,0:T(8,128)S(1)} %bitcast.20), custom_call_target="tpu_custom_call" | custom-call | flops 427819008 | bytes 1048576 | tf_op jit(solution)/shard_map/factor/pallas_call | solution.py:262
  (23 shorter events, 5.0 us)
Async XLA Ops:
  0.6 16.6 %collective-permute-start = (bf16[64,384]{1,0:T(8,128)(2,1)}, bf16[64,384]{1,0:T(8,128)(2,1)S(1)}, u32[]{:S(2)}, u32[]{:S(2)}) collective-permute-start(bf16[64,384]{1,0:T(8,128)(2,1)} %bitcast.25), channel_id=1, source_target_pairs={{0,16},{16,32},{32,48},{48,64},{64,80},{80,96},{96,112},{112,128},... | collective-permute-start | bytes 147464 | tf_op jit(solution)/shard_map/ppermute | solution.py:23
  7.3 1.4 %copy-start = (bf16[1,136,6144]{2,1,0:T(8,128)(2,1)S(1)}, bf16[1,136,6144]{2,1,0:T(8,128)(2,1)}, u32[]{:S(2)}) copy-start(bf16[1,136,6144]{2,1,0:T(8,128)(2,1)} %param.4) | copy-start | bytes 5013508
  8.7 8.5 %copy-start.5 = (bf16[1,384,64]{1,2,0:T(8,128)(2,1)S(1)}, bf16[1,384,64]{1,2,0:T(8,128)(2,1)}, u32[]{:S(2)}) copy-start(bf16[1,384,64]{1,2,0:T(8,128)(2,1)} %param.6) | copy-start | bytes 147460
  8.9 9.3 %collective-permute-start.1 = (bf16[8,136,384]{2,1,0:T(8,128)(2,1)S(1)}, bf16[8,136,384]{2,1,0:T(8,128)(2,1)S(1)}, u32[]{:S(2)}, u32[]{:S(2)}) collective-permute-start(bf16[8,136,384]{2,1,0:T(8,128)(2,1)S(1)} %get-tuple-element.22), channel_id=1, source_target_pairs={{0,1},{1,0},{2,3},{3,2},{4,5},{5,4},{6,7},{7,6},{8,9},{9,8},{10,11... | collective-permute-start | bytes 2506760 | tf_op jit(solution)/shard_map/ppermute | solution.py:27
  18.2 15.9 %all-to-all-start = ((bf16[8,128,384]{2,1,0:T(8,128)(2,1)}), bf16[8,128,384]{2,1,0:T(8,128)(2,1)S(1)}, u32[]{:S(2)}, u32[]{:S(2)}) async-start(bf16[8,128,384]{2,1,0:T(8,128)(2,1)} %copies.1), calls=%async_computation | async-start | bytes 1572864 | tf_op jit(solution)/shard_map/all_to_all | solution.py:35
  23.0 1.4 %copy-start.2 = (bf16[1,136,6144]{2,1,0:T(8,128)(2,1)S(1)}, bf16[1,136,6144]{2,1,0:T(8,128)(2,1)}, u32[]{:S(2)}) copy-start(bf16[1,136,6144]{2,1,0:T(8,128)(2,1)} %param.5) | copy-start | bytes 5013508
  24.6 5.8 %collective-permute-start.2 = (bf16[8,136,384]{2,1,0:T(8,128)(2,1)S(1)}, bf16[8,136,384]{2,1,0:T(8,128)(2,1)S(1)}, u32[]{:S(2)}, u32[]{:S(2)}) collective-permute-start(bf16[8,136,384]{2,1,0:T(8,128)(2,1)S(1)} %get-tuple-element.25), channel_id=1, source_target_pairs={{0,1},{1,0},{2,3},{3,2},{4,5},{5,4},{6,7},{7,6},{8,9},{9,8},{10,11... | collective-permute-start | bytes 2506760 | tf_op jit(solution)/shard_map/ppermute | solution.py:27
  30.4 0.9 copy-start.3
  39.2 8.7 %copy-start.1 = (bf16[1,136,6144]{2,1,0:T(8,128)(2,1)S(1)}, bf16[1,136,6144]{2,1,0:T(8,128)(2,1)}, u32[]{:S(2)}) copy-start(bf16[1,136,6144]{2,1,0:T(8,128)(2,1)} %param.4) | copy-start | bytes 5013508
  42.3 7.5 %collective-permute-start.3 = (bf16[208,128]{1,0:T(8,128)(2,1)S(1)}, bf16[208,128]{1,0:T(8,128)(2,1)S(1)}, u32[]{:S(2)}, u32[]{:S(2)}) collective-permute-start(bf16[208,128]{1,0:T(8,128)(2,1)S(1)} %factors_of.1.factors_ref), channel_id=1, source_target_pairs={{0,496},{16,0},{32,16},{48,32},{64,48},{80,64},{96,80},{112,96},{1... | collective-permute-start | bytes 159752 | tf_op jit(solution)/shard_map/ppermute | solution.py:23
  47.9 2.0 %copy-start.4 = (bf16[8,136,384]{2,1,0:T(8,128)(2,1)S(1)}, bf16[8,136,384]{2,1,0:T(8,128)(2,1)}, u32[]{:S(2)}) copy-start(bf16[8,136,384]{2,1,0:T(8,128)(2,1)} %copy-done.3) | copy-start | bytes 2506756
  75.4 8.8 %collective-permute-start.4 = (bf16[64,128]{1,0:T(8,128)(2,1)S(1)}, bf16[64,128]{1,0:T(8,128)(2,1)S(1)}, u32[]{:S(2)}, u32[]{:S(2)}) collective-permute-start(bf16[64,128]{1,0:T(8,128)(2,1)S(1)} %add_met.1), channel_id=1, source_target_pairs={{0,16},{16,32},{32,48},{48,64},{64,80},{80,96},{96,112},{112,128},... | collective-permute-start | bytes 49160 | tf_op jit(solution)/shard_map/ppermute | solution.py:23
  94.2 6.3 %collective-permute-start.5 = (bf16[64,384]{1,0:T(8,128)(2,1)S(1)}, bf16[64,384]{1,0:T(8,128)(2,1)S(1)}, u32[]{:S(2)}, u32[]{:S(2)}) collective-permute-start(bf16[64,384]{1,0:T(8,128)(2,1)S(1)} %add_up.1), channel_id=1, source_target_pairs={{0,496},{16,0},{32,16},{48,32},{64,48},{80,64},{96,80},{112,96},{1... | collective-permute-start | bytes 147464 | tf_op jit(solution)/shard_map/ppermute | solution.py:23

commit v7 on v6

--- a/solution.py
+++ b/solution.py
@@ -170,18 +170,18 @@
 
 def meet(whole_ref, terms_ref, out_ref):
     whole = side_by_side(whole_ref)
-    out_ref[:, : 2 * RANK] = lax.dot_general(whole, side_by_side(terms_ref), NT, preferred_element_type=F32)
-    out_ref[:, 2 * RANK : 3 * RANK] = lax.dot_general(whole, whole, NT, preferred_element_type=F32)
-    out_ref[:, 3 * RANK :] = jnp.zeros((RANK, RANK), F32)
+    out_ref[:RANK] = lax.dot_general(whole, side_by_side(terms_ref), NT, preferred_element_type=F32)
+    gram = lax.dot_general(whole, whole, NT, preferred_element_type=F32)
+    out_ref[RANK:] = jnp.concatenate([gram[:32], gram[32:]], axis=1)
 
 
 def add_met(parts_ref, out_ref):
-    out_ref[...] = (parts_ref[0, :, : 2 * RANK] + parts_ref[1, :, : 2 * RANK]).astype(BF16)
+    out_ref[...] = (parts_ref[0, :RANK] + parts_ref[1, :RANK]).astype(BF16)
 
 
 def factor(parts_ref, out_ref):
-    at = slice(2 * RANK, 3 * RANK)
-    out_ref[...] = inverse_cholesky(parts_ref[0, :, at] + parts_ref[1, :, at])
+    gram = parts_ref[0, RANK:] + parts_ref[1, RANK:]
+    out_ref[...] = inverse_cholesky(jnp.concatenate([gram[:, :RANK], gram[:, RANK:]], axis=0))
 
 
 def expand(met_ref, right_ref, out_ref):
@@ -252,7 +252,7 @@
     factors_in, rows_other, right, error = lax.optimization_barrier((factors_in, rows_other, right, error))
     terms, summed = kernel(project, stacked, blocks, flops=product)(core, rows_own, rows_other, factors_in)
     whole = across(kernel(add_and_copy, blocks)(across(summed)))
-    met = both_cores(kernel(meet, ((RANK, 256), F32), flops=product)(whole, terms))
+    met = both_cores(kernel(meet, ((96, 2 * RANK), F32), flops=product)(whole, terms))
     met_in = passed_along(kernel(add_met, ((RANK, 2 * RANK), BF16))(met), 1)
     met, error = lax.optimization_barrier((met, error))
     error = remainder(D // 2, core, micro, factors, error)

time: 103 us -> 103 us (level)
  no operation moved by 1% of the time
where the time goes in v7:
time: 103 us; the launch traced here: 101 us
  blocking collectives  38.3 us (37%)
  starting transfers between devices  31.2 us (30%)
  Pallas kernels  13.7 us (13%)
  waiting for transfers between devices  13.5 us (13%)
  local copies, waits for them, and re-layouts  3.79 us (4%)
    all_to_all x3, blocking collectives, across(): lax.all_to_all(blocks, 'dp', 0, 0, tiled=True, axis_index_groups=ACROSS)  29.2 us
    ppermute x4, starting transfers between devices, passed_along(): lax.ppermute(shard, 'pipe', [(i, (i + by) % devices) for i in range(devic...  18.5 us
    all_gather x2, blocking collectives, both_cores(): return lax.all_gather(shard, 'dp', axis_index_groups=CORES)  9.14 us
    ppermute x4, waiting for transfers between devices, passed_along(): lax.ppermute(shard, 'pipe', [(i, (i + by) % devices) for i in range(devic...  8.83 us
    ppermute x2, starting transfers between devices, exchanged(): return lax.ppermute(shard, 'dp', [(i, i ^ 1) for i in range(DP)])  7.92 us
    all_to_all x1, starting transfers between devices, across(): lax.all_to_all(blocks, 'dp', 0, 0, tiled=True, axis_index_groups=ACROSS)  4.82 us
    unnamed x12, local copies, waits for them, and re-layouts  3.79 us
    pallas_call x2, Pallas kernels, remainder(): pl.pallas_call(functools.partial(residual, first), out_shape=jax.ShapeDty...  3.19 us
  transfers between devices with their start and end apart: 7, of which 6 were waited for; matrix products, arithmetic and copies ran while one was open for 0% of the time, Pallas kernels for 7%

profile of v7, /device:TPU:1, one launch (start us, length us, event | category | flops | bytes accessed | tf_op | source)
XLA Modules:
  0.0 101.3 jit_solution(10399680321792446635)
XLA Ops:
  0.6 6.6 %collective-permute-start = (bf16[64,384]{1,0:T(8,128)(2,1)}, bf16[64,384]{1,0:T(8,128)(2,1)S(1)}, u32[]{:S(2)}, u32[]{:S(2)}) collective-permute-start(bf16[64,384]{1,0:T(8,128)(2,1)} %bitcast.25), channel_id=1, source_target_pairs={{0,16},{16,32},{32,48},{48,64},{64,80},{80,96},{96,112},{112,128},... | collective-permute-start | bytes 147464 | tf_op jit(solution)/shard_map/ppermute | solution.py:23
  7.3 1.4 %copy-done = bf16[1,136,6144]{2,1,0:T(8,128)(2,1)S(1)} copy-done((bf16[1,136,6144]{2,1,0:T(8,128)(2,1)S(1)}, bf16[1,136,6144]{2,1,0:T(8,128)(2,1)}, u32[]{:S(2)}) %copy-start) | copy-done | bytes 1671192
  8.9 4.1 %collective-permute-start.1 = (bf16[8,136,384]{2,1,0:T(8,128)(2,1)S(1)}, bf16[8,136,384]{2,1,0:T(8,128)(2,1)S(1)}, u32[]{:S(2)}, u32[]{:S(2)}) collective-permute-start(bf16[8,136,384]{2,1,0:T(8,128)(2,1)S(1)} %get-tuple-element.22), channel_id=1, source_target_pairs={{0,1},{1,0},{2,3},{3,2},{4,5},{5,4},{6,7},{7,6},{8,9},{9,8},{10,11... | collective-permute-start | bytes 2506760 | tf_op jit(solution)/shard_map/ppermute | solution.py:27
  13.0 4.3 %collective-permute-done.two_ref = bf16[64,384]{1,0:T(8,128)(2,1)S(1)} collective-permute-done((bf16[64,384]{1,0:T(8,128)(2,1)}, bf16[64,384]{1,0:T(8,128)(2,1)S(1)}, u32[]{:S(2)}, u32[]{:S(2)}) %collective-permute-start) | collective-permute-done | bytes 49184 | tf_op jit(solution)/shard_map/ppermute | solution.py:23
  17.2 0.9 copies.1
  18.2 4.8 %all-to-all-start = ((bf16[8,128,384]{2,1,0:T(8,128)(2,1)}), bf16[8,128,384]{2,1,0:T(8,128)(2,1)S(1)}, u32[]{:S(2)}, u32[]{:S(2)}) async-start(bf16[8,128,384]{2,1,0:T(8,128)(2,1)} %copies.1), calls=%async_computation | async-start | bytes 1572864 | tf_op jit(solution)/shard_map/all_to_all | solution.py:35
  23.0 1.4 %copy-done.2 = bf16[1,136,6144]{2,1,0:T(8,128)(2,1)S(1)} copy-done((bf16[1,136,6144]{2,1,0:T(8,128)(2,1)S(1)}, bf16[1,136,6144]{2,1,0:T(8,128)(2,1)}, u32[]{:S(2)}) %copy-start.2) | copy-done | bytes 1671192
  24.6 3.9 %collective-permute-start.2 = (bf16[8,136,384]{2,1,0:T(8,128)(2,1)S(1)}, bf16[8,136,384]{2,1,0:T(8,128)(2,1)S(1)}, u32[]{:S(2)}, u32[]{:S(2)}) collective-permute-start(bf16[8,136,384]{2,1,0:T(8,128)(2,1)S(1)} %get-tuple-element.25), channel_id=1, source_target_pairs={{0,1},{1,0},{2,3},{3,2},{4,5},{5,4},{6,7},{7,6},{8,9},{9,8},{10,11... | collective-permute-start | bytes 2506760 | tf_op jit(solution)/shard_map/ppermute | solution.py:27
  28.5 2.0 %collective-permute-done.2.other_ref = bf16[8,136,384]{2,1,0:T(8,128)(2,1)S(1)} collective-permute-done((bf16[8,136,384]{2,1,0:T(8,128)(2,1)S(1)}, bf16[8,136,384]{2,1,0:T(8,128)(2,1)S(1)}, u32[]{:S(2)}, u32[]{:S(2)}) %collective-permute-start.2) | collective-permute-done | bytes 835616 | tf_op jit(solution)/shard_map/ppermute | solution.py:27
  30.4 0.9 copy-done.3
  31.3 2.7 %all-to-all-done.both_ref = bf16[8,128,384]{2,1,0:T(8,128)(2,1)S(1)} async-done(((bf16[8,128,384]{2,1,0:T(8,128)(2,1)}), bf16[8,128,384]{2,1,0:T(8,128)(2,1)S(1)}, u32[]{:S(2)}, u32[]{:S(2)}) %all-to-all-start) | async-done | bytes 786464 | tf_op jit(solution)/shard_map/all_to_all | solution.py:35
  34.7 4.5 %all-gather = f32[4,136,128]{2,1,0:T(8,128)S(1)} all-gather(f32[2,136,128]{2,1,0:T(8,128)S(1)} %half_product.1), channel_id=2, replica_groups={{0,1},{2,3},{4,5},{6,7},{8,9},{10,11},{12,13},{14,15},{16,17},{18,19},{..., dimensions={0}, use_global_device_ids=true | all-gather | bytes 417792 | tf_op jit(solution)/shard_map/all_gather | solution.py:31
  39.2 3.1 %factors_of.1.factors_ref = bf16[208,128]{1,0:T(8,128)(2,1)S(1)} custom-call(f32[2,2,136,128]{3,2,1,0:T(8,128)S(1)} %bitcast.21), custom_call_target="tpu_custom_call" | custom-call | flops 427819008 | bytes 1048576 | tf_op jit(solution)/shard_map/factors_of/pallas_call | solution.py:248
  42.3 5.0 %collective-permute-start.3 = (bf16[208,128]{1,0:T(8,128)(2,1)S(1)}, bf16[208,128]{1,0:T(8,128)(2,1)S(1)}, u32[]{:S(2)}, u32[]{:S(2)}) collective-permute-start(bf16[208,128]{1,0:T(8,128)(2,1)S(1)} %factors_of.1.factors_ref), channel_id=1, source_target_pairs={{0,496},{16,0},{32,16},{48,32},{64,48},{80,64},{96,80},{112,96},{1... | collective-permute-start | bytes 159752 | tf_op jit(solution)/shard_map/ppermute | solution.py:23
  47.9 1.6 %residual.2.refs_0_ = bf16[136,6144]{1,0:T(8,128)(2,1)} custom-call(s32[1]{0:T(128)} %bitcast.core_ref, bf16[136,6144]{1,0:T(8,128)(2,1)S(1)} %bitcast.16, bf16[208,128]{1,0:T(8,128)(2,1)S(1)} %factors_of.1.factors_ref), custom_call_target="tpu_custom_call" | custom-call | flops 106954752 | bytes 1048576 | tf_op jit(solution)/shard_map/residual/pallas_call | solution.py:218
  50.6 10.1 %all_to_all.20.in_ref = bf16[8,64,384]{2,1,0:T(8,128)(2,1)S(1)} all-to-all(bf16[8,64,384]{2,1,0:T(8,128)(2,1)S(1)} %get-tuple-element.30), channel_id=1, replica_groups={{0,2,4,6,8,10,12,14},{1,3,5,7,9,11,13,15},{16,18,20,22,24,26,28,30},{17..., dimensions={0} | all-to-all | bytes 786432 | tf_op jit(solution)/shard_map/all_to_all | solution.py:35
  60.8 9.4 %all_to_all.21.whole_ref = bf16[8,64,384]{2,1,0:T(8,128)(2,1)S(1)} all-to-all(bf16[8,64,384]{2,1,0:T(8,128)(2,1)S(1)} %add_and_copy.1), channel_id=1, replica_groups={{0,2,4,6,8,10,12,14},{1,3,5,7,9,11,13,15},{16,18,20,22,24,26,28,30},{17..., dimensions={0} | all-to-all | bytes 786432 | tf_op jit(solution)/shard_map/all_to_all | solution.py:35
  70.8 4.6 %all-gather.1 = f32[192,128]{1,0:T(8,128)S(1)} all-gather(f32[96,128]{1,0:T(8,128)S(1)} %meet.1), channel_id=3, replica_groups={{0,1},{2,3},{4,5},{6,7},{8,9},{10,11},{12,13},{14,15},{16,17},{18,19},{..., dimensions={0}, use_global_device_ids=true | all-gather | bytes 147456 | tf_op jit(solution)/shard_map/all_gather | solution.py:31
  75.4 3.5 %collective-permute-start.4 = (bf16[64,128]{1,0:T(8,128)(2,1)S(1)}, bf16[64,128]{1,0:T(8,128)(2,1)S(1)}, u32[]{:S(2)}, u32[]{:S(2)}) collective-permute-start(bf16[64,128]{1,0:T(8,128)(2,1)S(1)} %add_met.1), channel_id=1, source_target_pairs={{0,16},{16,32},{32,48},{48,64},{64,80},{80,96},{96,112},{112,128},... | collective-permute-start | bytes 49160 | tf_op jit(solution)/shard_map/ppermute | solution.py:23
  79.0 1.6 %residual.3 = bf16[136,6144]{1,0:T(8,128)(2,1)} custom-call(s32[1]{0:T(128)} %bitcast.core_ref, bf16[136,6144]{1,0:T(8,128)(2,1)S(1)} %bitcast.17, bf16[208,128]{1,0:T(8,128)(2,1)S(1)} %factors_of.1.factors_ref, bf16[136,6144]{1,0:T(8,128)(2,1)} %residual.2.refs_0_), custom_call_target="tpu_custom_call", output_to_operand_aliasing={{}: (3, {})} | custom-call | flops 106954752 | bytes 1048576 | tf_op jit(solution)/shard_map/residual/pallas_call | solution.py:218
  80.6 3.6 %collective-permute-done.4.met_ref = bf16[64,128]{1,0:T(8,128)(2,1)S(1)} collective-permute-done((bf16[64,128]{1,0:T(8,128)(2,1)S(1)}, bf16[64,128]{1,0:T(8,128)(2,1)S(1)}, u32[]{:S(2)}, u32[]{:S(2)}) %collective-permute-start.4) | collective-permute-done | bytes 16416 | tf_op jit(solution)/shard_map/ppermute | solution.py:23
  84.5 9.6 %all_to_all.22.in_ref = bf16[8,64,384]{2,1,0:T(8,128)(2,1)S(1)} all-to-all(bf16[8,64,384]{2,1,0:T(8,128)(2,1)S(1)} %expand.1), channel_id=1, replica_groups={{0,2,4,6,8,10,12,14},{1,3,5,7,9,11,13,15},{16,18,20,22,24,26,28,30},{17..., dimensions={0} | all-to-all | bytes 786432 | tf_op jit(solution)/shard_map/all_to_all | solution.py:35
  94.2 3.3 %collective-permute-start.5 = (bf16[64,384]{1,0:T(8,128)(2,1)S(1)}, bf16[64,384]{1,0:T(8,128)(2,1)S(1)}, u32[]{:S(2)}, u32[]{:S(2)}) collective-permute-start(bf16[64,384]{1,0:T(8,128)(2,1)S(1)} %add_up.1), channel_id=1, source_target_pairs={{0,496},{16,0},{32,16},{48,32},{64,48},{80,64},{96,80},{112,96},{1... | collective-permute-start | bytes 147464 | tf_op jit(solution)/shard_map/ppermute | solution.py:23
  97.6 2.3 %factor.1.inverse_ref = f32[64,64]{1,0:T(8,128)S(1)} custom-call(f32[2,96,128]{2,1,0:T(8,128)S(1)} %bitcast.20), custom_call_target="tpu_custom_call" | custom-call | flops 427819008 | bytes 1048576 | tf_op jit(solution)/shard_map/factor/pallas_call | solution.py:262
  (23 shorter events, 5.1 us)
Async XLA Ops:
  0.6 16.6 %collective-permute-start = (bf16[64,384]{1,0:T(8,128)(2,1)}, bf16[64,384]{1,0:T(8,128)(2,1)S(1)}, u32[]{:S(2)}, u32[]{:S(2)}) collective-permute-start(bf16[64,384]{1,0:T(8,128)(2,1)} %bitcast.25), channel_id=1, source_target_pairs={{0,16},{16,32},{32,48},{48,64},{64,80},{80,96},{96,112},{112,128},... | collective-permute-start | bytes 147464 | tf_op jit(solution)/shard_map/ppermute | solution.py:23
  7.3 1.4 %copy-start = (bf16[1,136,6144]{2,1,0:T(8,128)(2,1)S(1)}, bf16[1,136,6144]{2,1,0:T(8,128)(2,1)}, u32[]{:S(2)}) copy-start(bf16[1,136,6144]{2,1,0:T(8,128)(2,1)} %param.4) | copy-start | bytes 5013508
  8.7 8.5 %copy-start.5 = (bf16[1,384,64]{1,2,0:T(8,128)(2,1)S(1)}, bf16[1,384,64]{1,2,0:T(8,128)(2,1)}, u32[]{:S(2)}) copy-start(bf16[1,384,64]{1,2,0:T(8,128)(2,1)} %param.6) | copy-start | bytes 147460
  8.9 9.3 %collective-permute-start.1 = (bf16[8,136,384]{2,1,0:T(8,128)(2,1)S(1)}, bf16[8,136,384]{2,1,0:T(8,128)(2,1)S(1)}, u32[]{:S(2)}, u32[]{:S(2)}) collective-permute-start(bf16[8,136,384]{2,1,0:T(8,128)(2,1)S(1)} %get-tuple-element.22), channel_id=1, source_target_pairs={{0,1},{1,0},{2,3},{3,2},{4,5},{5,4},{6,7},{7,6},{8,9},{9,8},{10,11... | collective-permute-start | bytes 2506760 | tf_op jit(solution)/shard_map/ppermute | solution.py:27
  18.2 15.9 %all-to-all-start = ((bf16[8,128,384]{2,1,0:T(8,128)(2,1)}), bf16[8,128,384]{2,1,0:T(8,128)(2,1)S(1)}, u32[]{:S(2)}, u32[]{:S(2)}) async-start(bf16[8,128,384]{2,1,0:T(8,128)(2,1)} %copies.1), calls=%async_computation | async-start | bytes 1572864 | tf_op jit(solution)/shard_map/all_to_all | solution.py:35
  23.0 1.4 %copy-start.2 = (bf16[1,136,6144]{2,1,0:T(8,128)(2,1)S(1)}, bf16[1,136,6144]{2,1,0:T(8,128)(2,1)}, u32[]{:S(2)}) copy-start(bf16[1,136,6144]{2,1,0:T(8,128)(2,1)} %param.5) | copy-start | bytes 5013508
  24.6 5.8 %collective-permute-start.2 = (bf16[8,136,384]{2,1,0:T(8,128)(2,1)S(1)}, bf16[8,136,384]{2,1,0:T(8,128)(2,1)S(1)}, u32[]{:S(2)}, u32[]{:S(2)}) collective-permute-start(bf16[8,136,384]{2,1,0:T(8,128)(2,1)S(1)} %get-tuple-element.25), channel_id=1, source_target_pairs={{0,1},{1,0},{2,3},{3,2},{4,5},{5,4},{6,7},{7,6},{8,9},{9,8},{10,11... | collective-permute-start | bytes 2506760 | tf_op jit(solution)/shard_map/ppermute | solution.py:27
  30.4 0.9 copy-start.3
  39.2 8.7 %copy-start.1 = (bf16[1,136,6144]{2,1,0:T(8,128)(2,1)S(1)}, bf16[1,136,6144]{2,1,0:T(8,128)(2,1)}, u32[]{:S(2)}) copy-start(bf16[1,136,6144]{2,1,0:T(8,128)(2,1)} %param.4) | copy-start | bytes 5013508
  42.3 7.5 %collective-permute-start.3 = (bf16[208,128]{1,0:T(8,128)(2,1)S(1)}, bf16[208,128]{1,0:T(8,128)(2,1)S(1)}, u32[]{:S(2)}, u32[]{:S(2)}) collective-permute-start(bf16[208,128]{1,0:T(8,128)(2,1)S(1)} %factors_of.1.factors_ref), channel_id=1, source_target_pairs={{0,496},{16,0},{32,16},{48,32},{64,48},{80,64},{96,80},{112,96},{1... | collective-permute-start | bytes 159752 | tf_op jit(solution)/shard_map/ppermute | solution.py:23
  47.9 2.0 %copy-start.4 = (bf16[8,136,384]{2,1,0:T(8,128)(2,1)S(1)}, bf16[8,136,384]{2,1,0:T(8,128)(2,1)}, u32[]{:S(2)}) copy-start(bf16[8,136,384]{2,1,0:T(8,128)(2,1)} %copy-done.3) | copy-start | bytes 2506756
  75.4 8.8 %collective-permute-start.4 = (bf16[64,128]{1,0:T(8,128)(2,1)S(1)}, bf16[64,128]{1,0:T(8,128)(2,1)S(1)}, u32[]{:S(2)}, u32[]{:S(2)}) collective-permute-start(bf16[64,128]{1,0:T(8,128)(2,1)S(1)} %add_met.1), channel_id=1, source_target_pairs={{0,16},{16,32},{32,48},{48,64},{64,80},{80,96},{96,112},{112,128},... | collective-permute-start | bytes 49160 | tf_op jit(solution)/shard_map/ppermute | solution.py:23
  94.2 6.3 %collective-permute-start.5 = (bf16[64,384]{1,0:T(8,128)(2,1)S(1)}, bf16[64,384]{1,0:T(8,128)(2,1)S(1)}, u32[]{:S(2)}, u32[]{:S(2)}) collective-permute-start(bf16[64,384]{1,0:T(8,128)(2,1)S(1)} %add_up.1), channel_id=1, source_target_pairs={{0,496},{16,0},{32,16},{48,32},{64,48},{80,64},{96,80},{112,96},{1... | collective-permute-start | bytes 147464 | tf_op jit(solution)/shard_map/ppermute | solution.py:23
